TPU v7x, 256 devices: a whole 4x4x8 slice. The times are simulated.
256 devices in a mesh: seq: 64 (over z, y_lo, x), dp: 4 (over y_hi, core).
Axes of the slice: x: 4, y: 4 (y_hi: 2, y_lo: 2; y = y_hi * 2 + y_lo), z: 8, core: 2. Of those that a mesh axis runs over, the one named last changes fastest.
Arguments:
- queries: bfloat16 [32768, 8192], P(('dp', 'seq')), parts along dimension 0, may hold values from -6 to 6
- keys: bfloat16 [32768, 1024], P(('dp', 'seq')), parts along dimension 0, may hold values from -6 to 6
- values: bfloat16 [32768, 1024], P(('dp', 'seq')), parts along dimension 0, may hold values from -6 to 6
- outputs: bfloat16 [32768, 8192], P(('dp', 'seq')), parts along dimension 0, may hold values from -6 to 6
- out_grad: bfloat16 [32768, 8192], P(('dp', 'seq')), parts along dimension 0, may hold values from -6 to 6
- lse: float32 [64, 32768], P(None, ('dp', 'seq')), parts along dimension 1, may hold values from 3 to 7
- segments: int32 [32768], P(('dp', 'seq')), parts along dimension 0, may hold values from 0 to 127, never falling along the last dimension, each value on 1 to 2048 neighbouring positions
Outputs:
- grad_queries: bfloat16 [32768, 8192], P(('dp', 'seq')), parts along dimension 0
- grad_keys: bfloat16 [32768, 1024], P(('dp', 'seq')), parts along dimension 0
- grad_values: bfloat16 [32768, 1024], P(('dp', 'seq')), parts along dimension 0
There are 4 independent parts, one for each index of `dp`. A program takes and returns all parts, laid end to end along the dimension named above; each array names one. Nothing has to cross between parts.
Inputs may be any that keep to these rules, and one draw needn't show every extreme that they name: `segments`: document ids never fall along the sequence; each document holds 1 to 2048 positions and one holds exactly 2048.
All inputs are finite; a program needn't handle non-finite values.
Results may differ from a plain program's by a relative error of at most 0.0055.
Values may be sent and summed in bfloat16 or wider, within the bound.
A program may use at most 128 MiB of HBM per device.

v0:
```python
import math

import jax
import jax.numpy as jnp
from jax import lax
from jax.sharding import PartitionSpec as P

HEAD_DIM = 128


def head_grads(q_heads, g_heads, k_cols_all, v_cols_all, lse_rows, delta_rows, seg_ids):
    head_count, length, head_width = q_heads.shape
    inv_root = 1.0 / math.sqrt(head_width)
    block_rows = min(512, length // 8)
    positions = jnp.arange(length, dtype=jnp.int32)

    def query_block(carried, block_index):
        row_start = block_index * block_rows
        q_rows = lax.dynamic_slice_in_dim(q_heads, row_start, block_rows, 1)
        g_rows = lax.dynamic_slice_in_dim(g_heads, row_start, block_rows, 1)
        lse_part = lax.dynamic_slice_in_dim(lse_rows, row_start, block_rows, 1)
        delta_part = lax.dynamic_slice_in_dim(delta_rows, row_start, block_rows, 1)
        seg_rows = lax.dynamic_slice_in_dim(seg_ids, row_start, block_rows, 0)
        pos_rows = lax.dynamic_slice_in_dim(positions, row_start, block_rows, 0)
        doc_first = jnp.min(jnp.where(seg_ids == seg_rows[0], positions, length))

        def tile_step(tile_index, loop_state):
            dq_block, dk_cols, dv_cols = loop_state
            col_start = (tile_index * block_rows).astype(jnp.int32)
            k_cols = lax.dynamic_slice_in_dim(k_cols_all, col_start, block_rows, 1)
            v_cols = lax.dynamic_slice_in_dim(v_cols_all, col_start, block_rows, 1)
            seg_cols = lax.dynamic_slice_in_dim(seg_ids, col_start, block_rows, 0)
            pos_cols = lax.dynamic_slice_in_dim(positions, col_start, block_rows, 0)
            scores = (
                jnp.einsum("hqd,dk->hqk", q_rows, k_cols, preferred_element_type=jnp.float32)
                * inv_root
            )
            visible = (seg_rows[:, None] == seg_cols[None, :]) & (
                pos_cols[None, :] <= pos_rows[:, None]
            )
            weights = jnp.where(visible[None], jnp.exp(scores - lse_part[:, :, None]), 0.0)
            d_weights = jnp.einsum(
                "hqd,dk->hqk", g_rows, v_cols, preferred_element_type=jnp.float32
            )
            dscore = (weights * (d_weights - delta_part[:, :, None])).astype(jnp.bfloat16)
            weights_low = weights.astype(jnp.bfloat16)
            dq_block = dq_block + inv_root * jnp.einsum(
                "hqk,dk->hqd", dscore, k_cols, preferred_element_type=jnp.float32
            )
            dk_tile = inv_root * jnp.einsum(
                "hqd,hqk->hdk", q_rows, dscore, preferred_element_type=jnp.float32
            )
            dv_tile = jnp.einsum(
                "hqd,hqk->hdk", g_rows, weights_low, preferred_element_type=jnp.float32
            )
            dk_cols = lax.dynamic_update_slice_in_dim(
                dk_cols,
                lax.dynamic_slice_in_dim(dk_cols, col_start, block_rows, 2) + dk_tile,
                col_start,
                2,
            )
            dv_cols = lax.dynamic_update_slice_in_dim(
                dv_cols,
                lax.dynamic_slice_in_dim(dv_cols, col_start, block_rows, 2) + dv_tile,
                col_start,
                2,
            )
            return (dq_block, dk_cols, dv_cols)

        start_state = (
            jnp.zeros((head_count, block_rows, head_width), jnp.float32),
            carried[0],
            carried[1],
        )
        loop_state = lax.fori_loop(doc_first // block_rows, block_index + 1, tile_step, start_state)
        return ((loop_state[1], loop_state[2]), loop_state[0].astype(jnp.bfloat16))

    zero_cols = jnp.zeros((head_count, head_width, length), jnp.float32)
    block_ids = jnp.arange(length // block_rows, dtype=jnp.int32)
    (dk_cols, dv_cols), dq_blocks = lax.scan(query_block, (zero_cols, zero_cols), block_ids)
    return (dq_blocks, dk_cols, dv_cols)


def on_device(queries, keys, values, outputs, out_grad, lse, segments):
    dev_rows = queries.shape[0]
    head_count = lse.shape[0]
    head_width = HEAD_DIM
    kv_heads = keys.shape[1] // head_width
    seq_size = lax.axis_size("seq")
    local_heads = head_count // seq_size
    group_size = head_count // kv_heads
    q_arrived, g_arrived = (
        lax.all_to_all(queries, "seq", split_axis=1, concat_axis=0, tiled=True),
        lax.all_to_all(out_grad, "seq", split_axis=1, concat_axis=0, tiled=True),
    )
    length = q_arrived.shape[0]
    q_heads = q_arrived.reshape(length, local_heads, head_width).transpose(1, 0, 2)
    g_heads = g_arrived.reshape(length, local_heads, head_width).transpose(1, 0, 2)
    all_ids = lax.all_gather(segments, "seq", axis=0, tiled=True)
    out_heads = lax.all_to_all(outputs, "seq", split_axis=1, concat_axis=0, tiled=True)
    lse_rows = lax.all_to_all(lse, "seq", split_axis=0, concat_axis=1, tiled=True)
    delta_rows = jnp.einsum(
        "lhd,hld->hl",
        out_heads.reshape(length, local_heads, head_width),
        g_heads,
        preferred_element_type=jnp.float32,
    )
    k_wide = jnp.broadcast_to(
        keys.reshape(dev_rows, kv_heads, 1, head_width),
        (dev_rows, kv_heads, group_size, head_width),
    ).reshape(dev_rows, head_count * head_width)
    v_wide = jnp.broadcast_to(
        values.reshape(dev_rows, kv_heads, 1, head_width),
        (dev_rows, kv_heads, group_size, head_width),
    ).reshape(dev_rows, head_count * head_width)
    k_arrived, v_arrived = (
        lax.all_to_all(k_wide, "seq", split_axis=1, concat_axis=0, tiled=True),
        lax.all_to_all(v_wide, "seq", split_axis=1, concat_axis=0, tiled=True),
    )
    k_cols_all = k_arrived.T
    v_cols_all = v_arrived.T
    dq_blocks, dk_cols, dv_cols = head_grads(
        q_heads, g_heads, k_cols_all, v_cols_all, lse_rows, delta_rows, all_ids
    )
    dq_rows = dq_blocks.transpose(0, 2, 1, 3).reshape(length, local_heads * head_width)
    grad_q = lax.all_to_all(dq_rows, "seq", split_axis=0, concat_axis=1, tiled=True)
    gradients = jnp.stack([dk_cols, dv_cols])
    returned = lax.all_to_all(
        gradients.reshape(2, local_heads * head_width, length),
        "seq",
        split_axis=2,
        concat_axis=1,
        tiled=True,
    )
    summed = returned.reshape(2, kv_heads, group_size, head_width, dev_rows).sum(axis=2)
    summed = summed.reshape(2, kv_heads * head_width, dev_rows).astype(jnp.bfloat16)
    return (grad_q, summed[0].T, summed[1].T)


def solution(mesh):
    in_specs = (
        P(("dp", "seq"), None),
        P(("dp", "seq"), None),
        P(("dp", "seq"), None),
        P(("dp", "seq"), None),
        P(("dp", "seq"), None),
        P(None, ("dp", "seq")),
        P(("dp", "seq")),
    )
    out_specs = (P(("dp", "seq"), None), P(("dp", "seq"), None), P(("dp", "seq"), None))
    return jax.shard_map(
        on_device, mesh=mesh, in_specs=in_specs, out_specs=out_specs, check_vma=False
    )
```

profile of v0, /device:TPU:96, one launch (start us, length us, event | category | flops | bytes accessed | tf_op | source)
XLA Modules:
  0.0 1124.5 jit_solution(12567753954575355369)
XLA Ops:
  0.6 11.9 %all-to-all-start.1 = ((f32[64,1,128]{2,1,0:T(1,128)}), f32[64,1,128]{2,1,0:T(1,128)S(1)}, u32[]{:S(2)}, u32[]{:S(2)}) async-start(f32[64,1,128]{2,1,0:T(1,128)} %bitcast.166), calls=%async_computation.1 | async-start | bytes 65536 | tf_op jit(solution)/shard_map/all_to_all | solution.py:101
  14.5 5.7 all-to-all-done.1
  20.2 8.2 all-to-all-start.2
  28.4 2.5 copy.36
  30.9 44.1 %all-to-all-done.2 = bf16[128,64,128]{2,0,1:T(8,128)(2,1)} async-done(((bf16[128,64,128]{2,0,1:T(8,128)(2,1)}), bf16[128,64,128]{2,0,1:T(8,128)(2,1)}, u32[]{:S(2)}, u32[]{:S(2)}) %all-to-all-start.2) | async-done | bytes 2097184 | tf_op jit(solution)/shard_map/all_to_all | solution.py:94
  75.0 9.6 all-to-all-start.3
  84.7 46.3 %all-to-all-done.3 = bf16[128,64,128]{0,2,1:T(8,128)(2,1)S(1)} async-done(((bf16[128,64,128]{0,2,1:T(8,128)(2,1)}), bf16[128,64,128]{0,2,1:T(8,128)(2,1)S(1)}, u32[]{:S(2)}, u32[]{:S(2)}) %all-to-all-start.3) | async-done | bytes 2097184 | tf_op jit(solution)/shard_map/all_to_all | solution.py:100
  132.9 9.8 all-to-all-start.4
  142.9 45.8 %all-to-all-done.4 = bf16[128,64,128]{0,2,1:T(8,128)(2,1)} async-done(((bf16[128,64,128]{0,2,1:T(8,128)(2,1)}), bf16[128,64,128]{0,2,1:T(8,128)(2,1)}, u32[]{:S(2)}, u32[]{:S(2)}) %all-to-all-start.4) | async-done | bytes 2097184 | tf_op jit(solution)/shard_map/all_to_all | solution.py:117
  190.6 9.7 all-to-all-start.5
  200.2 3.6 copy_bitcast_fusion.1
  203.8 41.9 %all-to-all-done.5 = bf16[128,64,128]{0,2,1:T(8,128)(2,1)} async-done(((bf16[128,64,128]{0,2,1:T(8,128)(2,1)}), bf16[128,64,128]{0,2,1:T(8,128)(2,1)}, u32[]{:S(2)}, u32[]{:S(2)}) %all-to-all-start.5) | async-done | bytes 2097184 | tf_op jit(solution)/shard_map/all_to_all | solution.py:118
  245.7 9.7 all-to-all-start
  255.4 174.9 %all-gather = s32[64,1,128]{2,1,0:T(1,128)S(1)} all-gather(s32[1,1,128]{2,1,0:T(1,128)S(1)} %bitcast.167), channel_id=1, replica_groups=mesh['seq'=64,'dp'=4] {'seq'}, dimensions={0}, use_global_device_ids=true | all-gather | bytes 33280 | tf_op jit(solution)/shard_map/all_gather | solution.py:99
  430.3 2.9 copy.59
  433.2 3.2 copy.39
  436.5 3.0 copy.42
  439.5 4.1 copy.41
  443.5 4.2 copy.43
  447.8 2.7 fusion.25
  450.6 2.2 broadcast_in_dim.45
  452.8 2.2 broadcast_in_dim.45.clone
  455.0 428.5 %while.44 = (s32[]{:T(128)}, f32[1,128,8192]{1,2,0:T(8,128)}, f32[1,128,8192]{1,2,0:T(8,128)}, bf16[16,1,512,128]{3,2,1,0:T(8,128)(2,1)}, s32[16]{0:T(128)S(1)},...) while((s32[]{:T(128)}, f32[1,128,8192]{1,2,0:T(8,128)}, ...), condition=%wide.region_4.5_spmd.clone, body=%wide.region_0.4_spmd.clone.sunk | while | flops 338583584 | bytes 8492404 | solution.py:80
  462.7 8.0 while.45
  479.0 16.0 %while.45 = (s32[]{:T(128)}, f32[1,512,128]{2,1,0:T(8,128)S(1)}, f32[1,128,8192]{1,2,0:T(8,128)}, f32[1,128,8192]{1,2,0:T(8,128)}, s32[]{:T(128)}, /*index=5*/s3...) while((s32[]{:T(128)}, f32[1,512,128]{2,1,0:T(8,128)S(1)}, ...), condition=%wide.region_3.3_spmd, body=%wide.region_2.2_spmd.sunk | while | flops 338493440 | bytes 7229687 | solution.py:75
  489.8 2.0 fusion.59
  503.4 16.0 %while.45 = (s32[]{:T(128)}, f32[1,512,128]{2,1,0:T(8,128)S(1)}, f32[1,128,8192]{1,2,0:T(8,128)}, f32[1,128,8192]{1,2,0:T(8,128)}, s32[]{:T(128)}, /*index=5*/s3...) while((s32[]{:T(128)}, f32[1,512,128]{2,1,0:T(8,128)S(1)}, ...), condition=%wide.region_3.3_spmd, body=%wide.region_2.2_spmd.sunk | while | flops 338493440 | bytes 7229687 | solution.py:75
  527.7 15.9 %while.45 = (s32[]{:T(128)}, f32[1,512,128]{2,1,0:T(8,128)S(1)}, f32[1,128,8192]{1,2,0:T(8,128)}, f32[1,128,8192]{1,2,0:T(8,128)}, s32[]{:T(128)}, /*index=5*/s3...) while((s32[]{:T(128)}, f32[1,512,128]{2,1,0:T(8,128)S(1)}, ...), condition=%wide.region_3.3_spmd, body=%wide.region_2.2_spmd.sunk | while | flops 338493440 | bytes 7229687 | solution.py:75
  552.0 15.9 %while.45 = (s32[]{:T(128)}, f32[1,512,128]{2,1,0:T(8,128)S(1)}, f32[1,128,8192]{1,2,0:T(8,128)}, f32[1,128,8192]{1,2,0:T(8,128)}, s32[]{:T(128)}, /*index=5*/s3...) while((s32[]{:T(128)}, f32[1,512,128]{2,1,0:T(8,128)S(1)}, ...), condition=%wide.region_3.3_spmd, body=%wide.region_2.2_spmd.sunk | while | flops 338493440 | bytes 7229687 | solution.py:75
  576.2 15.9 %while.45 = (s32[]{:T(128)}, f32[1,512,128]{2,1,0:T(8,128)S(1)}, f32[1,128,8192]{1,2,0:T(8,128)}, f32[1,128,8192]{1,2,0:T(8,128)}, s32[]{:T(128)}, /*index=5*/s3...) while((s32[]{:T(128)}, f32[1,512,128]{2,1,0:T(8,128)S(1)}, ...), condition=%wide.region_3.3_spmd, body=%wide.region_2.2_spmd.sunk | while | flops 338493440 | bytes 7229687 | solution.py:75
  600.5 15.9 %while.45 = (s32[]{:T(128)}, f32[1,512,128]{2,1,0:T(8,128)S(1)}, f32[1,128,8192]{1,2,0:T(8,128)}, f32[1,128,8192]{1,2,0:T(8,128)}, s32[]{:T(128)}, /*index=5*/s3...) while((s32[]{:T(128)}, f32[1,512,128]{2,1,0:T(8,128)S(1)}, ...), condition=%wide.region_3.3_spmd, body=%wide.region_2.2_spmd.sunk | while | flops 338493440 | bytes 7229687 | solution.py:75
  624.8 15.9 %while.45 = (s32[]{:T(128)}, f32[1,512,128]{2,1,0:T(8,128)S(1)}, f32[1,128,8192]{1,2,0:T(8,128)}, f32[1,128,8192]{1,2,0:T(8,128)}, s32[]{:T(128)}, /*index=5*/s3...) while((s32[]{:T(128)}, f32[1,512,128]{2,1,0:T(8,128)S(1)}, ...), condition=%wide.region_3.3_spmd, body=%wide.region_2.2_spmd.sunk | while | flops 338493440 | bytes 7229687 | solution.py:75
  649.1 15.9 %while.45 = (s32[]{:T(128)}, f32[1,512,128]{2,1,0:T(8,128)S(1)}, f32[1,128,8192]{1,2,0:T(8,128)}, f32[1,128,8192]{1,2,0:T(8,128)}, s32[]{:T(128)}, /*index=5*/s3...) while((s32[]{:T(128)}, f32[1,512,128]{2,1,0:T(8,128)S(1)}, ...), condition=%wide.region_3.3_spmd, body=%wide.region_2.2_spmd.sunk | while | flops 338493440 | bytes 7229687 | solution.py:75
  673.4 15.9 %while.45 = (s32[]{:T(128)}, f32[1,512,128]{2,1,0:T(8,128)S(1)}, f32[1,128,8192]{1,2,0:T(8,128)}, f32[1,128,8192]{1,2,0:T(8,128)}, s32[]{:T(128)}, /*index=5*/s3...) while((s32[]{:T(128)}, f32[1,512,128]{2,1,0:T(8,128)S(1)}, ...), condition=%wide.region_3.3_spmd, body=%wide.region_2.2_spmd.sunk | while | flops 338493440 | bytes 7229687 | solution.py:75
  697.6 16.0 %while.45 = (s32[]{:T(128)}, f32[1,512,128]{2,1,0:T(8,128)S(1)}, f32[1,128,8192]{1,2,0:T(8,128)}, f32[1,128,8192]{1,2,0:T(8,128)}, s32[]{:T(128)}, /*index=5*/s3...) while((s32[]{:T(128)}, f32[1,512,128]{2,1,0:T(8,128)S(1)}, ...), condition=%wide.region_3.3_spmd, body=%wide.region_2.2_spmd.sunk | while | flops 338493440 | bytes 7229687 | solution.py:75
  721.9 23.9 %while.45 = (s32[]{:T(128)}, f32[1,512,128]{2,1,0:T(8,128)S(1)}, f32[1,128,8192]{1,2,0:T(8,128)}, f32[1,128,8192]{1,2,0:T(8,128)}, s32[]{:T(128)}, /*index=5*/s3...) while((s32[]{:T(128)}, f32[1,512,128]{2,1,0:T(8,128)S(1)}, ...), condition=%wide.region_3.3_spmd, body=%wide.region_2.2_spmd.sunk | while | flops 338493440 | bytes 7229687 | solution.py:75
  754.2 31.9 %while.45 = (s32[]{:T(128)}, f32[1,512,128]{2,1,0:T(8,128)S(1)}, f32[1,128,8192]{1,2,0:T(8,128)}, f32[1,128,8192]{1,2,0:T(8,128)}, s32[]{:T(128)}, /*index=5*/s3...) while((s32[]{:T(128)}, f32[1,512,128]{2,1,0:T(8,128)S(1)}, ...), condition=%wide.region_3.3_spmd, body=%wide.region_2.2_spmd.sunk | while | flops 338493440 | bytes 7229687 | solution.py:75
  794.4 39.8 %while.45 = (s32[]{:T(128)}, f32[1,512,128]{2,1,0:T(8,128)S(1)}, f32[1,128,8192]{1,2,0:T(8,128)}, f32[1,128,8192]{1,2,0:T(8,128)}, s32[]{:T(128)}, /*index=5*/s3...) while((s32[]{:T(128)}, f32[1,512,128]{2,1,0:T(8,128)S(1)}, ...), condition=%wide.region_3.3_spmd, body=%wide.region_2.2_spmd.sunk | while | flops 338493440 | bytes 7229687 | solution.py:75
  842.6 15.9 %while.45 = (s32[]{:T(128)}, f32[1,512,128]{2,1,0:T(8,128)S(1)}, f32[1,128,8192]{1,2,0:T(8,128)}, f32[1,128,8192]{1,2,0:T(8,128)}, s32[]{:T(128)}, /*index=5*/s3...) while((s32[]{:T(128)}, f32[1,512,128]{2,1,0:T(8,128)S(1)}, ...), condition=%wide.region_3.3_spmd, body=%wide.region_2.2_spmd.sunk | while | flops 338493440 | bytes 7229687 | solution.py:75
  866.8 15.9 %while.45 = (s32[]{:T(128)}, f32[1,512,128]{2,1,0:T(8,128)S(1)}, f32[1,128,8192]{1,2,0:T(8,128)}, f32[1,128,8192]{1,2,0:T(8,128)}, s32[]{:T(128)}, /*index=5*/s3...) while((s32[]{:T(128)}, f32[1,512,128]{2,1,0:T(8,128)S(1)}, ...), condition=%wide.region_3.3_spmd, body=%wide.region_2.2_spmd.sunk | while | flops 338493440 | bytes 7229687 | solution.py:75
  883.5 21.7 %all-to-all-start.6 = ((bf16[64,128,128]{2,1,0:T(8,128)(2,1)}), bf16[64,128,128]{2,1,0:T(8,128)(2,1)S(1)}, u32[]{:S(2)}, u32[]{:S(2)}) async-start(bf16[64,128,128]{2,1,0:T(8,128)(2,1)} %bitcast.156), calls=%async_computation.6 | async-start | bytes 4194304 | tf_op jit(solution)/shard_map/all_to_all | solution.py:126
  905.2 10.0 maximum_bitcast_fusion
  915.1 37.0 %all-to-all-done.6 = bf16[64,128,128]{2,1,0:T(8,128)(2,1)S(1)} async-done(((bf16[64,128,128]{2,1,0:T(8,128)(2,1)}), bf16[64,128,128]{2,1,0:T(8,128)(2,1)S(1)}, u32[]{:S(2)}, u32[]{:S(2)}) %all-to-all-start.6) | async-done | bytes 2097184 | tf_op jit(solution)/shard_map/all_to_all | solution.py:126
  952.2 15.2 %all-to-all-start.7 = ((f32[2,128,8192]{1,0,2:T(2,128)}), f32[2,128,8192]{1,0,2:T(2,128)}, u32[]{:S(2)}, u32[]{:S(2)}) async-start(f32[2,128,8192]{1,0,2:T(2,128)} %maximum_bitcast_fusion), calls=%async_computation.7 | async-start | bytes 16777216 | tf_op jit(solution)/shard_map/all_to_all | solution.py:128
  967.4 2.9 copy.44
  970.4 4.1 copy.48
  974.4 139.4 %all-to-all-done.7 = f32[2,128,8192]{1,0,2:T(2,128)} async-done(((f32[2,128,8192]{1,0,2:T(2,128)}), f32[2,128,8192]{1,0,2:T(2,128)}, u32[]{:S(2)}, u32[]{:S(2)}) %all-to-all-start.7) | async-done | bytes 8388640 | tf_op jit(solution)/shard_map/all_to_all | solution.py:128
  1113.8 8.5 reduce.1
  (431 shorter events, 367.0 us)
Async XLA Ops:
  0.6 11.9 %copy-start = (bf16[128,8192]{1,0:T(8,128)(2,1)S(1)}, bf16[128,8192]{1,0:T(8,128)(2,1)}, u32[]{:S(2)}) copy-start(bf16[128,8192]{1,0:T(8,128)(2,1)} %param.15) | copy-start | bytes 6291460
  0.6 19.6 %all-to-all-start.1 = ((f32[64,1,128]{2,1,0:T(1,128)}), f32[64,1,128]{2,1,0:T(1,128)S(1)}, u32[]{:S(2)}, u32[]{:S(2)}) async-start(f32[64,1,128]{2,1,0:T(1,128)} %bitcast.166), calls=%async_computation.1 | async-start | bytes 65536 | tf_op jit(solution)/shard_map/all_to_all | solution.py:101
  14.5 13.9 %copy-start.3 = (bf16[128,8192]{1,0:T(8,128)(2,1)S(1)}, bf16[128,8192]{1,0:T(8,128)(2,1)}, u32[]{:S(2)}) copy-start(bf16[128,8192]{1,0:T(8,128)(2,1)} %param.14) | copy-start | bytes 6291460
  20.2 54.8 %all-to-all-start.2 = ((bf16[128,64,128]{2,0,1:T(8,128)(2,1)}), bf16[128,64,128]{2,0,1:T(8,128)(2,1)}, u32[]{:S(2)}, u32[]{:S(2)}) async-start(bf16[128,64,128]{2,0,1:T(8,128)(2,1)} %copy_bitcast_fusion), calls=%async_computation.2 | async-start | bytes 4194304 | tf_op jit(solution)/shard_map/all_to_all | solution.py:94
  75.0 9.6 copy-start.4
  75.0 56.1 %all-to-all-start.3 = ((bf16[128,64,128]{0,2,1:T(8,128)(2,1)}), bf16[128,64,128]{0,2,1:T(8,128)(2,1)S(1)}, u32[]{:S(2)}, u32[]{:S(2)}) async-start(bf16[128,64,128]{0,2,1:T(8,128)(2,1)} %bitcast.150), calls=%async_computation.3 | async-start | bytes 4194304 | tf_op jit(solution)/shard_map/all_to_all | solution.py:100
  132.9 9.8 copy-start.5
  132.9 55.8 %all-to-all-start.4 = ((bf16[128,64,128]{0,2,1:T(8,128)(2,1)}), bf16[128,64,128]{0,2,1:T(8,128)(2,1)}, u32[]{:S(2)}, u32[]{:S(2)}) async-start(bf16[128,64,128]{0,2,1:T(8,128)(2,1)} %bitcast.151), calls=%async_computation.4 | async-start | bytes 4194304 | tf_op jit(solution)/shard_map/all_to_all | solution.py:117
  190.6 55.1 %all-to-all-start.5 = ((bf16[128,64,128]{0,2,1:T(8,128)(2,1)}), bf16[128,64,128]{0,2,1:T(8,128)(2,1)}, u32[]{:S(2)}, u32[]{:S(2)}) async-start(bf16[128,64,128]{0,2,1:T(8,128)(2,1)} %bitcast.152), calls=%async_computation.5 | async-start | bytes 4194304 | tf_op jit(solution)/shard_map/all_to_all | solution.py:118
  203.8 51.6 %copy-start.6 = (s32[128]{0:T(128)S(1)}, s32[128]{0:T(128)}, u32[]{:S(2)}) copy-start(s32[128]{0:T(128)} %param.17) | copy-start | bytes 1540
  245.7 204.8 %all-to-all-start = ((bf16[128,64,128]{2,0,1:T(8,128)(2,1)}), bf16[128,64,128]{2,0,1:T(8,128)(2,1)}, u32[]{:S(2)}, u32[]{:S(2)}) async-start(bf16[128,64,128]{2,0,1:T(8,128)(2,1)} %copy_bitcast_fusion.1), calls=%async_computation | async-start | bytes 4194304 | tf_op jit(solution)/shard_map/all_to_all | solution.py:93
  443.5 4.2 copy-start.2
  883.5 68.7 %all-to-all-start.6 = ((bf16[64,128,128]{2,1,0:T(8,128)(2,1)}), bf16[64,128,128]{2,1,0:T(8,128)(2,1)S(1)}, u32[]{:S(2)}, u32[]{:S(2)}) async-start(bf16[64,128,128]{2,1,0:T(8,128)(2,1)} %bitcast.156), calls=%async_computation.6 | async-start | bytes 4194304 | tf_op jit(solution)/shard_map/all_to_all | solution.py:126
  952.2 161.6 %all-to-all-start.7 = ((f32[2,128,8192]{1,0,2:T(2,128)}), f32[2,128,8192]{1,0,2:T(2,128)}, u32[]{:S(2)}, u32[]{:S(2)}) async-start(f32[2,128,8192]{1,0,2:T(2,128)} %maximum_bitcast_fusion), calls=%async_computation.7 | async-start | bytes 16777216 | tf_op jit(solution)/shard_map/all_to_all | solution.py:128
  1113.8 10.7 copy-start.1
where the time goes:
time: 1130 us; the launch traced here: 1120 us
  waiting for transfers between devices  360 us (32%)
  matrix products  287 us (25%)
  blocking collectives  175 us (15%)
  starting transfers between devices  95.7 us (8%)
  local copies, waits for them, and re-layouts  85.2 us (8%)
  loops' own time  67.7 us (6%)
  other arithmetic  52.4 us (5%)
    all_gather x1, blocking collectives, on_device(): all_ids = lax.all_gather(segments, 'seq', axis=0, tiled=True)  175 us
    all_to_all x1, waiting for transfers between devices, on_device(): lax.all_to_all(gradients.reshape(2, local_heads * head_width, length), 's...  139 us
    dot_general x37, matrix products, tile_step(): jnp.einsum('hqd,hqk->hdk', q_rows, dscore, preferred_element_type=jnp.flo...  72.3 us
    dot_general x37, matrix products, tile_step(): jnp.einsum('hqd,hqk->hdk', g_rows, weights_low, preferred_element_type=jn...  72.3 us
    another operation x1, loops' own time, head_grads(): lax.scan(query_block, (zero_cols, zero_cols), block_ids)  65.8 us
    dot_general x37, matrix products, tile_step(): jnp.einsum('hqd,dk->hqk', q_rows, k_cols, preferred_element_type=jnp.floa...  50.7 us
    dot_general x37, matrix products, tile_step(): jnp.einsum('hqk,dk->hqd', dscore, k_cols, preferred_element_type=jnp.floa...  46.6 us
    all_to_all x1, waiting for transfers between devices, on_device(): lax.all_to_all(outputs, 'seq', split_axis=1, concat_axis=0, tiled=True)  46.3 us
  transfers between devices with their start and end apart: 8, of which 7 were waited for; matrix products, arithmetic and copies ran while one was open for 4% of the time, Pallas kernels for 0%

commit v1 on v0

v1 whole, which is shorter than its diff:
```python
import functools
import math

import jax
import jax.numpy as jnp
from jax import lax
from jax.experimental import pallas as pl
from jax.experimental.pallas import tpu as pltpu
from jax.sharding import PartitionSpec as P

D = 128
LOG2E = math.log2(math.e)
MESH = pl.DeviceIdType.MESH
PLANE = 8
HALO = 2
BLOCK = 256


def dev(index):
    return {"seq": index}


def greet(me, plane, rank, planes):
    barrier = pltpu.get_barrier_semaphore()
    for o in range(1, PLANE):
        peer = plane * PLANE + lax.rem(rank + o, PLANE)
        pl.semaphore_signal(barrier, inc=1, device_id=dev(peer), device_id_type=MESH)
    count = PLANE - 1
    for dz in range(1, HALO + 1):
        up = plane + dz < planes
        down = plane >= dz

        @pl.when(up)
        def _():
            pl.semaphore_signal(barrier, inc=1, device_id=dev(me + dz * PLANE), device_id_type=MESH)

        @pl.when(down)
        def _():
            pl.semaphore_signal(barrier, inc=1, device_id=dev(me - dz * PLANE), device_id_type=MESH)

        count = count + up.astype(jnp.int32) + down.astype(jnp.int32)
    pl.semaphore_wait(barrier, count)


def gather_kernel(
    planes, q, g, k, v, lse, delta, seg, q_all, g_all, k_win, v_win, lse_all, delta_all, seg_win,
    send, recv, z_send, z_recv, local,
):
    rows = q.shape[0]
    span = rows * PLANE
    wide = q_all.shape[1]
    heads = lse_all.shape[0]
    me = lax.axis_index("seq")
    plane, rank = me // PLANE, lax.rem(me, PLANE)

    def cols(index, width):
        return pl.ds(pl.multiple_of(index * width, width), width)

    own = HALO * span

    pieces = [
        (lambda p: seg, lambda s: seg_win.at[:, pl.ds(pl.multiple_of(own + s * rows, rows), rows)]),
        (lambda p: k.at[:, cols(p, D)], lambda s: k_win.at[pl.ds(pl.multiple_of(own + s * rows, rows), rows), :]),
        (lambda p: v.at[:, cols(p, D)], lambda s: v_win.at[pl.ds(pl.multiple_of(own + s * rows, rows), rows), :]),
        (lambda p: lse.at[cols(p, heads), :], lambda s: lse_all.at[:, cols(s, rows)]),
        (lambda p: delta.at[cols(p, heads), :], lambda s: delta_all.at[:, cols(s, rows)]),
        (lambda p: q.at[:, cols(p, wide)], lambda s: q_all.at[cols(s, rows), :]),
        (lambda p: g.at[:, cols(p, wide)], lambda s: g_all.at[cols(s, rows), :]),
    ]

    def own_copy(n):
        source, target = pieces[n]
        return pltpu.make_async_copy(source(rank), target(rank), local.at[n])

    def plane_copy(n, o):
        source, target = pieces[n]
        peer = lax.rem(rank + o, PLANE)
        return pltpu.make_async_remote_copy(
            source(peer), target(rank), send.at[n, o - 1], recv.at[n, o - 1],
            device_id=dev(plane * PLANE + peer), device_id_type=MESH,
        )

    def arrival(n, o):
        source, target = pieces[n]
        origin = lax.rem(rank + PLANE - o, PLANE)
        return pltpu.make_async_remote_copy(
            source(rank), target(origin), send.at[n, o - 1], recv.at[n, o - 1],
            device_id=dev(plane * PLANE + origin), device_id_type=MESH,
        )

    def z_copy(n, dz):
        if n == 0:
            whole = seg_win.at[:, pl.ds(own, span)]
            there = seg_win.at[:, pl.ds(own - dz * span, span)]
        else:
            win = (k_win, v_win)[n - 1]
            whole = win.at[pl.ds(own, span), :]
            there = win.at[pl.ds(own - dz * span, span), :]
        return pltpu.make_async_remote_copy(
            whole, there, z_send.at[n, dz - 1], z_recv.at[n, dz - 1],
            device_id=dev(me + dz * PLANE), device_id_type=MESH,
        )

    greet(me, plane, rank, planes)
    for n in range(len(pieces)):
        for o in range(1, PLANE):
            plane_copy(n, o).start()
        own_copy(n).start()
    for n in range(3):
        own_copy(n).wait()
        for o in range(1, PLANE):
            arrival(n, o).wait_recv()
        for dz in range(1, HALO + 1):
            @pl.when(plane + dz < planes)
            def _():
                z_copy(n, dz).start()
    for n in range(3, len(pieces)):
        own_copy(n).wait()
        for o in range(1, PLANE):
            arrival(n, o).wait_recv()
    for n in range(len(pieces)):
        for o in range(1, PLANE):
            plane_copy(n, o).wait_send()
    for n in range(3):
        for dz in range(1, HALO + 1):
            @pl.when(plane + dz < planes)
            def _():
                z_copy(n, dz).wait_send()

            @pl.when(plane >= dz)
            def _():
                z_copy(n, dz).wait_recv()


def gather(q, g, k, v, lse, delta, seg, planes):
    rows = q.shape[0]
    span = rows * PLANE
    heads = lse.shape[0] // PLANE
    window = (HALO + 1) * span
    any_space = pl.BlockSpec(memory_space=pl.ANY)
    return pl.pallas_call(
        functools.partial(gather_kernel, planes),
        out_shape=(
            jax.ShapeDtypeStruct((span, heads * D), q.dtype),
            jax.ShapeDtypeStruct((span, heads * D), g.dtype),
            jax.ShapeDtypeStruct((window, D), k.dtype),
            jax.ShapeDtypeStruct((window, D), v.dtype),
            jax.ShapeDtypeStruct((heads, span), lse.dtype),
            jax.ShapeDtypeStruct((heads, span), delta.dtype),
            jax.ShapeDtypeStruct((seg.shape[0], window), seg.dtype),
        ),
        in_specs=[any_space] * 7,
        out_specs=(any_space,) * 7,
        scratch_shapes=[
            pltpu.SemaphoreType.DMA((7, PLANE - 1)),
            pltpu.SemaphoreType.DMA((7, PLANE - 1)),
            pltpu.SemaphoreType.DMA((3, HALO)),
            pltpu.SemaphoreType.DMA((3, HALO)),
            pltpu.SemaphoreType.DMA((7,)),
        ],
        compiler_params=pltpu.CompilerParams(collective_id=0, has_side_effects=True),
        name="gather_plane",
    )(q, g, k, v, lse, delta, seg)


def attend_kernel(
    bounds, start, lse, delta, q, g, k, v, dq, dk_halo, dv_halo, dk_own, dv_own, dk, dv, k_t
):
    head = pl.program_id(0)
    span = q.shape[0]
    own = k.shape[0] - span
    inv_root = 1.0 / math.sqrt(D)
    scale = inv_root * LOG2E

    @pl.when(head == 0)
    def _():
        dk[...] = jnp.zeros_like(dk)
        dv[...] = jnp.zeros_like(dv)
        k_t[...] = k[...].T

    @pl.loop(0, span // BLOCK)
    def _(i):
        here = pl.ds(pl.multiple_of(i * BLOCK, BLOCK), BLOCK)
        q_rows, g_rows = q[here, :], g[here, :]
        lse_row = lse[0, :, here] * LOG2E
        delta_row = delta[0, :, here]
        start_row = start[:, here]

        def tile(masked, j, dq_t):
            there = pl.ds(pl.multiple_of(j * BLOCK, BLOCK), BLOCK)
            k_rows, v_rows = k[there, :], v[there, :]
            nt = (((1,), (1,)), ((), ()))
            scores = lax.dot_general(k_rows, q_rows, nt, preferred_element_type=jnp.float32)
            weights = jnp.exp2(scores * scale - lse_row)
            if masked:
                key_at = j * BLOCK + lax.broadcasted_iota(jnp.int32, (BLOCK, BLOCK), 0)
                query_at = own + i * BLOCK + lax.broadcasted_iota(jnp.int32, (BLOCK, BLOCK), 1)
                weights = jnp.where((key_at >= start_row) & (key_at <= query_at), weights, 0.0)
            d_weights = lax.dot_general(v_rows, g_rows, nt, preferred_element_type=jnp.float32)
            dscore = (weights * (d_weights - delta_row)).astype(jnp.bfloat16)
            low = weights.astype(jnp.bfloat16)
            dv[there, :] += jnp.dot(low, g_rows, preferred_element_type=jnp.float32)
            dk[there, :] += jnp.dot(dscore, q_rows, preferred_element_type=jnp.float32)
            return dq_t + jnp.dot(k_t[:, there], dscore, preferred_element_type=jnp.float32)

        diagonal = own // BLOCK + i
        low_end, full = bounds[0, i], bounds[1, i]
        dq_t = jnp.zeros((D, BLOCK), jnp.float32)
        dq_t = lax.fori_loop(low_end, full, functools.partial(tile, True), dq_t)
        dq_t = lax.fori_loop(full, diagonal, functools.partial(tile, False), dq_t)
        dq_t = tile(True, diagonal, dq_t)
        dq[here, :] = (dq_t.T * inv_root).astype(dq.dtype)

    @pl.when(head == pl.num_programs(0) - 1)
    def _():
        dk_halo[...] = (dk[:own, :] * inv_root).astype(dk_halo.dtype)
        dv_halo[...] = dv[:own, :].astype(dv_halo.dtype)
        dk_own[...] = dk[own:, :] * inv_root
        dv_own[...] = dv[own:, :]


def attend(q, g, k, v, lse, delta, seg_win, planes):
    span = q.shape[0]
    heads = q.shape[1] // D
    window = k.shape[0]
    own = window - span
    plane = lax.axis_index("seq") // PLANE
    at = jnp.arange(window, dtype=jnp.int32)
    ids = jnp.where(at >= own - plane * span, seg_win[0], -1)
    own_ids = ids[own:]
    start = jnp.sum((ids[None, :] < own_ids[:, None]).astype(jnp.int32), axis=1)
    tiles = span // BLOCK
    edge = start.reshape(tiles, BLOCK)
    diagonal = own // BLOCK + jnp.arange(tiles, dtype=jnp.int32)
    low_end = edge[:, 0] // BLOCK
    full = jnp.minimum((edge[:, -1] + BLOCK - 1) // BLOCK, diagonal)
    bounds = jnp.stack([low_end, jnp.maximum(full, low_end)])
    column = pl.BlockSpec((span, D), lambda h, b: (0, h))
    row = pl.BlockSpec((1, 1, span), lambda h, b: (h, 0, 0))

    def whole(shape):
        return pl.BlockSpec(shape, lambda h, b: (0, 0))

    return pl.pallas_call(
        attend_kernel,
        grid_spec=pltpu.PrefetchScalarGridSpec(
            num_scalar_prefetch=1,
            grid=(heads,),
            in_specs=[whole((1, span)), row, row, column, column, whole((window, D)), whole((window, D))],
            out_specs=[column, whole((own, D)), whole((own, D)), whole((span, D)), whole((span, D))],
            scratch_shapes=[
                pltpu.VMEM((window, D), jnp.float32),
                pltpu.VMEM((window, D), jnp.float32),
                pltpu.VMEM((D, window), jnp.bfloat16),
            ],
        ),
        out_shape=(
            jax.ShapeDtypeStruct((span, heads * D), q.dtype),
            jax.ShapeDtypeStruct((own, D), jnp.bfloat16),
            jax.ShapeDtypeStruct((own, D), jnp.bfloat16),
            jax.ShapeDtypeStruct((span, D), jnp.float32),
            jax.ShapeDtypeStruct((span, D), jnp.float32),
        ),
        compiler_params=pltpu.CompilerParams(vmem_limit_bytes=48 * 1024 * 1024),
        name="attend",
    )(bounds, start[None, :], lse[:, None, :], delta[:, None, :], q, g, k, v)


def scatter_kernel(
    planes, dq, dk_halo, dv_halo, dk_own, dv_own, grad_q, grad_k, grad_v,
    dk_in, dv_in, dk_low, dv_low, total, send, recv, z_send, z_recv, last_send, last_recv, local,
):
    rows = grad_q.shape[0]
    span = rows * PLANE
    wide = dq.shape[1]
    me = lax.axis_index("seq")
    plane, rank = me // PLANE, lax.rem(me, PLANE)

    def cols(index, width):
        return pl.ds(pl.multiple_of(index * width, width), width)

    def z_copy(n, dz):
        halo, into = ((dk_halo, dk_in), (dv_halo, dv_in))[n]
        return pltpu.make_async_remote_copy(
            halo.at[pl.ds((HALO - dz) * span, span), :], into.at[dz - 1],
            z_send.at[n, dz - 1], z_recv.at[n, dz - 1],
            device_id=dev(me - dz * PLANE), device_id_type=MESH,
        )

    def q_copy(o, origin):
        peer = lax.rem(rank + o, PLANE)
        return pltpu.make_async_remote_copy(
            dq.at[cols(peer, rows), :], grad_q.at[:, cols(origin, wide)], send.at[o - 1], recv.at[o - 1],
            device_id=dev(plane * PLANE + peer), device_id_type=MESH,
        )

    def kv_copy(n, o, origin):
        low, out = ((dk_low, grad_k), (dv_low, grad_v))[n]
        peer = lax.rem(rank + o, PLANE)
        return pltpu.make_async_remote_copy(
            low.at[cols(peer, rows), :], out.at[:, cols(origin, D)], last_send.at[n, o - 1], last_recv.at[n, o - 1],
            device_id=dev(plane * PLANE + peer), device_id_type=MESH,
        )

    greet(me, plane, rank, planes)
    for n in range(2):
        for dz in range(1, HALO + 1):
            @pl.when(plane >= dz)
            def _():
                z_copy(n, dz).start()
    for o in range(1, PLANE):
        q_copy(o, rank).start()
    own_q = pltpu.make_async_copy(dq.at[cols(rank, rows), :], grad_q.at[:, cols(rank, wide)], local.at[0])
    own_q.start()
    own_kv = []
    for n in range(2):
        low, out, own, into = ((dk_low, grad_k, dk_own, dk_in), (dv_low, grad_v, dv_own, dv_in))[n]
        total[...] = own[...]
        for dz in range(1, HALO + 1):
            @pl.when(plane + dz < planes)
            def _():
                z_copy(n, dz).wait_recv()
                total[...] += into[dz - 1].astype(jnp.float32)
        low[...] = total[...].astype(low.dtype)
        for o in range(1, PLANE):
            kv_copy(n, o, rank).start()
        own_kv.append(pltpu.make_async_copy(low.at[cols(rank, rows), :], out.at[:, cols(rank, D)], local.at[1 + n]))
        own_kv[n].start()
    own_q.wait()
    for n in range(2):
        own_kv[n].wait()
        for dz in range(1, HALO + 1):
            @pl.when(plane >= dz)
            def _():
                z_copy(n, dz).wait_send()
    for o in range(1, PLANE):
        origin = lax.rem(rank + PLANE - o, PLANE)
        q_copy(o, origin).wait()
        for n in range(2):
            kv_copy(n, o, origin).wait()


def scatter(dq, dk_halo, dv_halo, dk_own, dv_own, planes):
    span, wide = dq.shape
    rows = span // PLANE
    any_space = pl.BlockSpec(memory_space=pl.ANY)
    vmem = pl.BlockSpec(memory_space=pltpu.VMEM)
    return pl.pallas_call(
        functools.partial(scatter_kernel, planes),
        out_shape=(
            jax.ShapeDtypeStruct((rows, PLANE * wide), dq.dtype),
            jax.ShapeDtypeStruct((rows, PLANE * D), jnp.bfloat16),
            jax.ShapeDtypeStruct((rows, PLANE * D), jnp.bfloat16),
        ),
        in_specs=[any_space] * 3 + [vmem] * 2,
        out_specs=(any_space,) * 3,
        scratch_shapes=[
            pltpu.VMEM((HALO, span, D), jnp.bfloat16),
            pltpu.VMEM((HALO, span, D), jnp.bfloat16),
            pltpu.VMEM((span, D), jnp.bfloat16),
            pltpu.VMEM((span, D), jnp.bfloat16),
            pltpu.VMEM((span, D), jnp.float32),
            pltpu.SemaphoreType.DMA((PLANE - 1,)),
            pltpu.SemaphoreType.DMA((PLANE - 1,)),
            pltpu.SemaphoreType.DMA((2, HALO)),
            pltpu.SemaphoreType.DMA((2, HALO)),
            pltpu.SemaphoreType.DMA((2, PLANE - 1)),
            pltpu.SemaphoreType.DMA((2, PLANE - 1)),
            pltpu.SemaphoreType.DMA((3,)),
        ],
        compiler_params=pltpu.CompilerParams(
            collective_id=1, has_side_effects=True, vmem_limit_bytes=32 * 1024 * 1024
        ),
        name="scatter_plane",
    )(dq, dk_halo, dv_halo, dk_own, dv_own)


def on_device(queries, keys, values, outputs, out_grad, lse, segments):
    rows = queries.shape[0]
    heads = lse.shape[0]
    planes = lax.axis_size("seq") // PLANE
    delta = jnp.sum(
        (outputs.astype(jnp.float32) * out_grad.astype(jnp.float32)).reshape(rows, heads, D), axis=2
    ).T
    seg = jnp.broadcast_to(segments[None, :], (8, rows))
    q, g, k, v, lse_all, delta_all, seg_win = gather(
        queries, out_grad, keys, values, lse, delta, seg, planes
    )
    dq, dk_halo, dv_halo, dk_own, dv_own = attend(q, g, k, v, lse_all, delta_all, seg_win, planes)
    return scatter(dq, dk_halo, dv_halo, dk_own, dv_own, planes)


def solution(mesh):
    rows = P(("dp", "seq"), None)
    in_specs = (rows, rows, rows, rows, rows, P(None, ("dp", "seq")), P(("dp", "seq")))
    return jax.shard_map(
        on_device, mesh=mesh, in_specs=in_specs, out_specs=(rows, rows, rows), check_vma=False
    )
```

time: 1130 us -> 234 us (0.21)
  the two profiles are of different devices: /device:TPU:96 before, /device:TPU:48 now
where the time goes in v1:
time: 234 us; the launch traced here: 233 us
  Pallas kernels  213 us (91%)
  local copies, waits for them, and re-layouts  11.2 us (5%)
  other arithmetic  8.56 us (4%)
    pallas_call x1, Pallas kernels, scatter(): pl.pallas_call(functools.partial(scatter_kernel, planes), out_shape=(jax....  85.7 us
    pallas_call x1, Pallas kernels, gather(): pl.pallas_call(functools.partial(gather_kernel, planes), out_shape=(jax.S...  72.8 us
    pallas_call x1, Pallas kernels, attend(): pl.pallas_call(attend_kernel, grid_spec=pltpu.PrefetchScalarGridSpec(num_...  54.4 us
    unnamed x8, local copies, waits for them, and re-layouts  7.65 us

profile of v1, /device:TPU:48, one launch (start us, length us, event | category | flops | bytes accessed | tf_op | source)
XLA Modules:
  0.0 233.4 jit_solution(1996312188314994332)
XLA Ops:
  0.6 1.2 broadcast_in_dim.23.seg
  1.9 2.7 %multiply_bitcast_fusion = f32[16,8,64,128]{3,1,2,0:T(8,128)S(1)} fusion(bf16[128,8192]{1,0:T(8,128)(2,1)} %g.1, bf16[128,8192]{1,0:T(8,128)(2,1)} %param.10), kind=kLoop, calls=%fused_computation.1 | loop fusion | flops 3145728 | bytes 8388608
  4.6 2.7 %copy.12 = f32[16,8,64,128]{3,2,1,0:T(8,128)} copy(f32[16,8,64,128]{3,1,2,0:T(8,128)S(1)} %multiply_bitcast_fusion) | data formatting | bytes 8388608
  7.3 3.3 %reduce_sum.18 = f32[128,64]{1,0:T(8,128)S(1)} reduce(f32[128,64,128]{2,1,0:T(8,128)} %bitcast.28, f32[]{:T(128)} %constant.52.clone.1), dimensions={2}, to_apply=%region_0.0 | reduce | flops 1040384 | bytes 4227076 | tf_op jit(solution)/shard_map/reduce_sum | solution.py:382
  10.6 0.7 copy.11
  11.3 72.8 %gather_plane.1 = (bf16[1024,1024]{1,0:T(8,128)(2,1)}, bf16[1024,1024]{1,0:T(8,128)(2,1)}, bf16[3072,128]{1,0:T(8,128)(2,1)}, bf16[3072,128]{1,0:T(8,128)(2,1)},...) custom-call(bf16[128,8192]{1,0:T(8,128)(2,1)} %q.1, bf16[128,8192]{1,0:T(8,128)(2,1)} %g.1, ...), custom_call_target="tpu_custom_call" | custom-call | tf_op jit(solution)/shard_map/gather_plane/pallas_call | solution.py:141
  84.2 0.9 fusion.1
  85.1 1.4 convert_reduce_fusion
  86.5 0.2 slice_reduce_fusion
  86.7 0.8 broadcast_in_dim.27.lse
  87.5 0.8 broadcast_in_dim.28.delta
  88.3 0.0 copy-start
  88.3 1.1 copy-done
  89.4 0.0 copy-start.1
  89.4 1.1 copy-done.1
  90.5 54.4 %attend.1 = (bf16[1024,1024]{1,0:T(8,128)(2,1)S(1)}, bf16[2048,128]{1,0:T(8,128)(2,1)S(1)}, bf16[2048,128]{1,0:T(8,128)(2,1)S(1)}, f32[1024,128]{1,0:T(8,128)S(1)}, f32[1024,128]{1,0:T(8,128)S(1)}) custom-call(s32[2,4]{1,0:T(2,128)S(1)} %pad_add_fusion.bounds, s32[1,1024]{1,0:T(1,128)S(1)} %bitcast.27, f32[8,1,1024]{2,1,0:T(1,128)S(1)} %broadcast_in_dim.27.lse, ...), custom_call_target="tpu_custom_call" | custom-call | tf_op jit(solution)/shard_map/attend/pallas_call | solution.py:244
  145.0 85.7 %scatter_plane.1 = (bf16[128,8192]{1,0:T(8,128)(2,1)S(1)}, bf16[128,1024]{1,0:T(8,128)(2,1)S(1)}, bf16[128,1024]{1,0:T(8,128)(2,1)S(1)}) custom-call(bf16[1024,1024]{1,0:T(8,128)(2,1)S(1)} %get-tuple-element.22.dq, bf16[2048,128]{1,0:T(8,128)(2,1)S(1)} %get-tuple-element.23.dk_halo, bf16[2048,128]{1,0:T(8,128)(2,1)S(1)} %get-tuple-element.24.dv_halo, ...), custom_call_target="tpu_custom_call" | custom-call | tf_op jit(solution)/shard_map/scatter_plane/pallas_call | solution.py:348
  230.7 1.3 copy.16
  232.0 0.7 copy.17
  232.7 0.7 copy.18
  (4 shorter events, 0.0 us)
Async XLA Ops:
  88.3 1.1 copy-start
  89.4 1.1 copy-start.1

commit v2 on v1

--- a/solution.py
+++ b/solution.py
@@ -14,6 +14,7 @@
 PLANE = 8
 HALO = 2
 BLOCK = 256
+VMEM_LIMIT = 60 * 1024 * 1024
 
 
 def dev(index):
@@ -43,30 +44,32 @@
 
 
 def gather_kernel(
-    planes, q, g, k, v, lse, delta, seg, q_all, g_all, k_win, v_win, lse_all, delta_all, seg_win,
-    send, recv, z_send, z_recv, local,
+    planes, q, g, o, k, v, seg, lse, q_all, g_all, k_win, v_win, stats_all, seg_win,
+    o_here, g_here, stats, seg_here, send, recv, z_send, z_recv, local,
 ):
     rows = q.shape[0]
     span = rows * PLANE
     wide = q_all.shape[1]
-    heads = lse_all.shape[0]
+    heads = wide // D
     me = lax.axis_index("seq")
     plane, rank = me // PLANE, lax.rem(me, PLANE)
-
-    def cols(index, width):
+    own = HALO * span
+
+    def part(index, width):
         return pl.ds(pl.multiple_of(index * width, width), width)
 
-    own = HALO * span
+    def own_part(s):
+        return pl.ds(pl.multiple_of(own + s * rows, rows), rows)
 
     pieces = [
-        (lambda p: seg, lambda s: seg_win.at[:, pl.ds(pl.multiple_of(own + s * rows, rows), rows)]),
-        (lambda p: k.at[:, cols(p, D)], lambda s: k_win.at[pl.ds(pl.multiple_of(own + s * rows, rows), rows), :]),
-        (lambda p: v.at[:, cols(p, D)], lambda s: v_win.at[pl.ds(pl.multiple_of(own + s * rows, rows), rows), :]),
-        (lambda p: lse.at[cols(p, heads), :], lambda s: lse_all.at[:, cols(s, rows)]),
-        (lambda p: delta.at[cols(p, heads), :], lambda s: delta_all.at[:, cols(s, rows)]),
-        (lambda p: q.at[:, cols(p, wide)], lambda s: q_all.at[cols(s, rows), :]),
-        (lambda p: g.at[:, cols(p, wide)], lambda s: g_all.at[cols(s, rows), :]),
+        (lambda p: seg_here, lambda s: seg_win.at[:, own_part(s)]),
+        (lambda p: k.at[:, part(p, D)], lambda s: k_win.at[own_part(s), :]),
+        (lambda p: v.at[:, part(p, D)], lambda s: v_win.at[own_part(s), :]),
+        (lambda p: q.at[:, part(p, wide)], lambda s: q_all.at[part(s, rows), :]),
+        (lambda p: g.at[:, part(p, wide)], lambda s: g_all.at[part(s, rows), :]),
+        (lambda p: stats.at[part(p, 2 * heads), :], lambda s: stats_all.at[:, part(s, rows)]),
     ]
+    last = len(pieces) - 1
 
     def own_copy(n):
         source, target = pieces[n]
@@ -101,26 +104,49 @@
             device_id=dev(me + dz * PLANE), device_id_type=MESH,
         )
 
+    load_o = pltpu.make_async_copy(o, o_here, local.at[last + 1])
+    load_g = pltpu.make_async_copy(g, g_here, local.at[last + 2])
+    load_o.start()
+    load_g.start()
+    seg_here[...] = jnp.broadcast_to(seg[...], seg_here.shape)
     greet(me, plane, rank, planes)
-    for n in range(len(pieces)):
-        for o in range(1, PLANE):
-            plane_copy(n, o).start()
+    for n in range(last):
+        for o_at in range(1, PLANE):
+            plane_copy(n, o_at).start()
         own_copy(n).start()
+
+    load_o.wait()
+    load_g.wait()
+
+    @pl.loop(0, PLANE)
+    def _(p):
+        sums = []
+        for h in range(heads):
+            features = pl.ds(pl.multiple_of(p * wide + h * D, D), D)
+            product = o_here[:, features].astype(jnp.float32) * g_here[:, features].astype(jnp.float32)
+            sums.append(jnp.sum(product.T, axis=0, keepdims=True))
+        stats[pl.ds(pl.multiple_of(p * 2 * heads, heads), heads), :] = lse[pl.ds(pl.multiple_of(p * heads, heads), heads), :]
+        stats[pl.ds(pl.multiple_of((p * 2 + 1) * heads, heads), heads), :] = jnp.concatenate(sums, axis=0)
+
+    for o_at in range(1, PLANE):
+        plane_copy(last, o_at).start()
+    own_copy(last).start()
+
     for n in range(3):
         own_copy(n).wait()
-        for o in range(1, PLANE):
-            arrival(n, o).wait_recv()
+        for o_at in range(1, PLANE):
+            arrival(n, o_at).wait_recv()
         for dz in range(1, HALO + 1):
             @pl.when(plane + dz < planes)
             def _():
                 z_copy(n, dz).start()
-    for n in range(3, len(pieces)):
+    for n in range(3, last + 1):
         own_copy(n).wait()
-        for o in range(1, PLANE):
-            arrival(n, o).wait_recv()
-    for n in range(len(pieces)):
-        for o in range(1, PLANE):
-            plane_copy(n, o).wait_send()
+        for o_at in range(1, PLANE):
+            arrival(n, o_at).wait_recv()
+    for n in range(last + 1):
+        for o_at in range(1, PLANE):
+            plane_copy(n, o_at).wait_send()
     for n in range(3):
         for dz in range(1, HALO + 1):
             @pl.when(plane + dz < planes)
@@ -132,12 +158,13 @@
                 z_copy(n, dz).wait_recv()
 
 
-def gather(q, g, k, v, lse, delta, seg, planes):
+def gather(q, g, o, k, v, seg, lse, planes):
     rows = q.shape[0]
     span = rows * PLANE
     heads = lse.shape[0] // PLANE
     window = (HALO + 1) * span
     any_space = pl.BlockSpec(memory_space=pl.ANY)
+    vmem = pl.BlockSpec(memory_space=pltpu.VMEM)
     return pl.pallas_call(
         functools.partial(gather_kernel, planes),
         out_shape=(
@@ -145,73 +172,100 @@
             jax.ShapeDtypeStruct((span, heads * D), g.dtype),
             jax.ShapeDtypeStruct((window, D), k.dtype),
             jax.ShapeDtypeStruct((window, D), v.dtype),
-            jax.ShapeDtypeStruct((heads, span), lse.dtype),
-            jax.ShapeDtypeStruct((heads, span), delta.dtype),
-            jax.ShapeDtypeStruct((seg.shape[0], window), seg.dtype),
+            jax.ShapeDtypeStruct((2 * heads, span), lse.dtype),
+            jax.ShapeDtypeStruct((8, window), seg.dtype),
         ),
-        in_specs=[any_space] * 7,
-        out_specs=(any_space,) * 7,
+        in_specs=[any_space] * 5 + [vmem] * 2,
+        out_specs=(any_space,) * 6,
         scratch_shapes=[
-            pltpu.SemaphoreType.DMA((7, PLANE - 1)),
-            pltpu.SemaphoreType.DMA((7, PLANE - 1)),
+            pltpu.VMEM(o.shape, o.dtype),
+            pltpu.VMEM(g.shape, g.dtype),
+            pltpu.VMEM((2 * heads * PLANE, rows), jnp.float32),
+            pltpu.VMEM((8, rows), jnp.int32),
+            pltpu.SemaphoreType.DMA((6, PLANE - 1)),
+            pltpu.SemaphoreType.DMA((6, PLANE - 1)),
             pltpu.SemaphoreType.DMA((3, HALO)),
             pltpu.SemaphoreType.DMA((3, HALO)),
-            pltpu.SemaphoreType.DMA((7,)),
+            pltpu.SemaphoreType.DMA((8,)),
         ],
-        compiler_params=pltpu.CompilerParams(collective_id=0, has_side_effects=True),
+        compiler_params=pltpu.CompilerParams(
+            collective_id=0, has_side_effects=True, vmem_limit_bytes=VMEM_LIMIT
+        ),
         name="gather_plane",
-    )(q, g, k, v, lse, delta, seg)
+    )(q, g, o, k, v, seg, lse)
 
 
 def attend_kernel(
-    bounds, start, lse, delta, q, g, k, v, dq, dk_halo, dv_halo, dk_own, dv_own, dk, dv, k_t
+    seg, stats, q, g, k, v, dq, dk_halo, dv_halo, dk_own, dv_own, dk, dv, k_t, start
 ):
-    head = pl.program_id(0)
-    span = q.shape[0]
-    own = k.shape[0] - span
+    i = pl.program_id(0)
+    window = k.shape[0]
+    span = dk_own.shape[0]
+    own = window - span
+    heads = q.shape[1] // D
+    across = heads * BLOCK
     inv_root = 1.0 / math.sqrt(D)
     scale = inv_root * LOG2E
 
-    @pl.when(head == 0)
+    @pl.when(i == 0)
     def _():
         dk[...] = jnp.zeros_like(dk)
         dv[...] = jnp.zeros_like(dv)
         k_t[...] = k[...].T
-
-    @pl.loop(0, span // BLOCK)
-    def _(i):
-        here = pl.ds(pl.multiple_of(i * BLOCK, BLOCK), BLOCK)
-        q_rows, g_rows = q[here, :], g[here, :]
-        lse_row = lse[0, :, here] * LOG2E
-        delta_row = delta[0, :, here]
-        start_row = start[:, here]
-
-        def tile(masked, j, dq_t):
-            there = pl.ds(pl.multiple_of(j * BLOCK, BLOCK), BLOCK)
-            k_rows, v_rows = k[there, :], v[there, :]
-            nt = (((1,), (1,)), ((), ()))
-            scores = lax.dot_general(k_rows, q_rows, nt, preferred_element_type=jnp.float32)
-            weights = jnp.exp2(scores * scale - lse_row)
-            if masked:
-                key_at = j * BLOCK + lax.broadcasted_iota(jnp.int32, (BLOCK, BLOCK), 0)
-                query_at = own + i * BLOCK + lax.broadcasted_iota(jnp.int32, (BLOCK, BLOCK), 1)
-                weights = jnp.where((key_at >= start_row) & (key_at <= query_at), weights, 0.0)
-            d_weights = lax.dot_general(v_rows, g_rows, nt, preferred_element_type=jnp.float32)
-            dscore = (weights * (d_weights - delta_row)).astype(jnp.bfloat16)
-            low = weights.astype(jnp.bfloat16)
-            dv[there, :] += jnp.dot(low, g_rows, preferred_element_type=jnp.float32)
-            dk[there, :] += jnp.dot(dscore, q_rows, preferred_element_type=jnp.float32)
-            return dq_t + jnp.dot(k_t[:, there], dscore, preferred_element_type=jnp.float32)
-
-        diagonal = own // BLOCK + i
-        low_end, full = bounds[0, i], bounds[1, i]
-        dq_t = jnp.zeros((D, BLOCK), jnp.float32)
-        dq_t = lax.fori_loop(low_end, full, functools.partial(tile, True), dq_t)
-        dq_t = lax.fori_loop(full, diagonal, functools.partial(tile, False), dq_t)
-        dq_t = tile(True, diagonal, dq_t)
-        dq[here, :] = (dq_t.T * inv_root).astype(dq.dtype)
-
-    @pl.when(head == pl.num_programs(0) - 1)
+        ids = seg[...]
+        at = lax.broadcasted_iota(jnp.int32, ids.shape, 1)
+        plane = lax.axis_index("seq") // PLANE
+        first = own - jnp.minimum(plane, HALO) * span
+        begins = (ids != pltpu.roll(ids, 1, 1)) & (at > first)
+        found = jnp.where(begins, at, first)
+        step = 1
+        while step < window:
+            found = jnp.where(at >= step, jnp.maximum(found, pltpu.roll(found, step, 1)), found)
+            step *= 2
+        start[...] = found[:, own:]
+
+    def stacked(ref):
+        return jnp.concatenate([ref[:, h * D:(h + 1) * D] for h in range(heads)], axis=0)
+
+    def in_line(first):
+        return jnp.concatenate([stats[first + h:first + h + 1, :] for h in range(heads)], axis=1)
+
+    q_rows, g_rows = stacked(q), stacked(g)
+    lse_row = in_line(0) * LOG2E
+    delta_row = in_line(heads)
+    block_start = start[0:1, pl.ds(pl.multiple_of(i * BLOCK, BLOCK), BLOCK)]
+    start_row = jnp.concatenate([block_start] * heads, axis=1)
+    query_row = own + i * BLOCK + lax.rem(lax.broadcasted_iota(jnp.int32, (1, across), 1), BLOCK)
+
+    def tile(masked, j, dq_t):
+        there = pl.ds(pl.multiple_of(j * BLOCK, BLOCK), BLOCK)
+        k_rows, v_rows = k[there, :], v[there, :]
+        nt = (((1,), (1,)), ((), ()))
+        scores = lax.dot_general(k_rows, q_rows, nt, preferred_element_type=jnp.float32)
+        weights = jnp.exp2(scores * scale - lse_row)
+        if masked:
+            key_at = j * BLOCK + lax.broadcasted_iota(jnp.int32, (BLOCK, across), 0)
+            weights = jnp.where((key_at >= start_row) & (key_at <= query_row), weights, 0.0)
+        d_weights = lax.dot_general(v_rows, g_rows, nt, preferred_element_type=jnp.float32)
+        dscore = (weights * (d_weights - delta_row)).astype(jnp.bfloat16)
+        low = weights.astype(jnp.bfloat16)
+        dv[there, :] += jnp.dot(low, g_rows, preferred_element_type=jnp.float32)
+        dk[there, :] += jnp.dot(dscore, q_rows, preferred_element_type=jnp.float32)
+        return dq_t + jnp.dot(k_t[:, there], dscore, preferred_element_type=jnp.float32)
+
+    position = block_start.astype(jnp.float32)
+    diagonal = own // BLOCK + i
+    low_end = jnp.min(position).astype(jnp.int32) // BLOCK
+    full = (jnp.max(position).astype(jnp.int32) + BLOCK - 1) // BLOCK
+    full = jnp.clip(full, low_end, diagonal)
+    dq_t = jnp.zeros((D, across), jnp.float32)
+    dq_t = lax.fori_loop(low_end, full, functools.partial(tile, True), dq_t)
+    dq_t = lax.fori_loop(full, diagonal, functools.partial(tile, False), dq_t)
+    dq_t = tile(True, diagonal, dq_t)
+    for h in range(heads):
+        dq[:, h * D:(h + 1) * D] = (dq_t[:, h * BLOCK:(h + 1) * BLOCK].T * inv_root).astype(dq.dtype)
+
+    @pl.when(i == pl.num_programs(0) - 1)
     def _():
         dk_halo[...] = (dk[:own, :] * inv_root).astype(dk_halo.dtype)
         dv_halo[...] = dv[:own, :].astype(dv_halo.dtype)
@@ -219,51 +273,39 @@
         dv_own[...] = dv[own:, :]
 
 
-def attend(q, g, k, v, lse, delta, seg_win, planes):
-    span = q.shape[0]
-    heads = q.shape[1] // D
+def attend(q, g, k, v, stats, seg_win):
+    span, wide = q.shape
     window = k.shape[0]
     own = window - span
-    plane = lax.axis_index("seq") // PLANE
-    at = jnp.arange(window, dtype=jnp.int32)
-    ids = jnp.where(at >= own - plane * span, seg_win[0], -1)
-    own_ids = ids[own:]
-    start = jnp.sum((ids[None, :] < own_ids[:, None]).astype(jnp.int32), axis=1)
-    tiles = span // BLOCK
-    edge = start.reshape(tiles, BLOCK)
-    diagonal = own // BLOCK + jnp.arange(tiles, dtype=jnp.int32)
-    low_end = edge[:, 0] // BLOCK
-    full = jnp.minimum((edge[:, -1] + BLOCK - 1) // BLOCK, diagonal)
-    bounds = jnp.stack([low_end, jnp.maximum(full, low_end)])
-    column = pl.BlockSpec((span, D), lambda h, b: (0, h))
-    row = pl.BlockSpec((1, 1, span), lambda h, b: (h, 0, 0))
+    block = pl.BlockSpec((BLOCK, wide), lambda i: (i, 0))
 
     def whole(shape):
-        return pl.BlockSpec(shape, lambda h, b: (0, 0))
+        return pl.BlockSpec(shape, lambda i: (0, 0))
 
     return pl.pallas_call(
         attend_kernel,
-        grid_spec=pltpu.PrefetchScalarGridSpec(
-            num_scalar_prefetch=1,
-            grid=(heads,),
-            in_specs=[whole((1, span)), row, row, column, column, whole((window, D)), whole((window, D))],
-            out_specs=[column, whole((own, D)), whole((own, D)), whole((span, D)), whole((span, D))],
-            scratch_shapes=[
-                pltpu.VMEM((window, D), jnp.float32),
-                pltpu.VMEM((window, D), jnp.float32),
-                pltpu.VMEM((D, window), jnp.bfloat16),
-            ],
-        ),
+        grid=(span // BLOCK,),
+        in_specs=[
+            whole(seg_win.shape), pl.BlockSpec((stats.shape[0], BLOCK), lambda i: (0, i)),
+            block, block, whole((window, D)), whole((window, D)),
+        ],
+        out_specs=[block, whole((own, D)), whole((own, D)), whole((span, D)), whole((span, D))],
         out_shape=(
-            jax.ShapeDtypeStruct((span, heads * D), q.dtype),
+            jax.ShapeDtypeStruct((span, wide), q.dtype),
             jax.ShapeDtypeStruct((own, D), jnp.bfloat16),
             jax.ShapeDtypeStruct((own, D), jnp.bfloat16),
             jax.ShapeDtypeStruct((span, D), jnp.float32),
             jax.ShapeDtypeStruct((span, D), jnp.float32),
         ),
-        compiler_params=pltpu.CompilerParams(vmem_limit_bytes=48 * 1024 * 1024),
+        scratch_shapes=[
+            pltpu.VMEM((window, D), jnp.float32),
+            pltpu.VMEM((window, D), jnp.float32),
+            pltpu.VMEM((D, window), jnp.bfloat16),
+            pltpu.VMEM((8, span), jnp.int32),
+        ],
+        compiler_params=pltpu.CompilerParams(vmem_limit_bytes=VMEM_LIMIT),
         name="attend",
-    )(bounds, start[None, :], lse[:, None, :], delta[:, None, :], q, g, k, v)
+    )(seg_win, stats, q, g, k, v)
 
 
 def scatter_kernel(
@@ -369,25 +411,18 @@
             pltpu.SemaphoreType.DMA((3,)),
         ],
         compiler_params=pltpu.CompilerParams(
-            collective_id=1, has_side_effects=True, vmem_limit_bytes=32 * 1024 * 1024
+            collective_id=1, has_side_effects=True, vmem_limit_bytes=VMEM_LIMIT
         ),
         name="scatter_plane",
     )(dq, dk_halo, dv_halo, dk_own, dv_own)
 
 
 def on_device(queries, keys, values, outputs, out_grad, lse, segments):
-    rows = queries.shape[0]
-    heads = lse.shape[0]
     planes = lax.axis_size("seq") // PLANE
-    delta = jnp.sum(
-        (outputs.astype(jnp.float32) * out_grad.astype(jnp.float32)).reshape(rows, heads, D), axis=2
-    ).T
-    seg = jnp.broadcast_to(segments[None, :], (8, rows))
-    q, g, k, v, lse_all, delta_all, seg_win = gather(
-        queries, out_grad, keys, values, lse, delta, seg, planes
+    q, g, k, v, stats, seg_win = gather(
+        queries, out_grad, outputs, keys, values, segments[None, :], lse, planes
     )
-    dq, dk_halo, dv_halo, dk_own, dv_own = attend(q, g, k, v, lse_all, delta_all, seg_win, planes)
-    return scatter(dq, dk_halo, dv_halo, dk_own, dv_own, planes)
+    return scatter(*attend(q, g, k, v, stats, seg_win), planes)
 
 
 def solution(mesh):

time: 234 us -> 167 us (0.71)
  the two profiles are of different devices: /device:TPU:48 before, /device:TPU:96 now
where the time goes in v2:
time: 167 us; the launch traced here: 165 us
  Pallas kernels  159 us (95%)
  local copies, waits for them, and re-layouts  4.56 us (3%)
    pallas_call x1, Pallas kernels, gather(): pl.pallas_call(functools.partial(gather_kernel, planes), out_shape=(jax.S...  74.8 us
    pallas_call x1, Pallas kernels, scatter(): pl.pallas_call(functools.partial(scatter_kernel, planes), out_shape=(jax....  64.1 us
    pallas_call x1, Pallas kernels, attend(): pl.pallas_call(attend_kernel, grid=(span // BLOCK,), in_specs=[whole(seg_...  20.5 us
    unnamed x7, local copies, waits for them, and re-layouts  4.56 us

profile of v2, /device:TPU:96, one launch (start us, length us, event | category | flops | bytes accessed | tf_op | source)
XLA Modules:
  0.0 164.6 jit_solution(9686439746788259535)
XLA Ops:
  0.6 74.8 %gather_plane.1 = (bf16[1024,1024]{1,0:T(8,128)(2,1)}, bf16[1024,1024]{1,0:T(8,128)(2,1)}, bf16[3072,128]{1,0:T(8,128)(2,1)}, bf16[3072,128]{1,0:T(8,128)(2,1)}, f32[16,1024]{1,0:T(8,128)}, /*index=5*/s32[8,3072]{1,0:T(8,128)}) custom-call(bf16[128,8192]{1,0:T(8,128)(2,1)} %q.1, bf16[128,8192]{1,0:T(8,128)(2,1)} %g.1, bf16[128,8192]{1,0:T(8,128)(2,1)} %o.1, ...), custom_call_target="tpu_custom_call" | custom-call | tf_op jit(solution)/shard_map/gather_plane/pallas_call | solution.py:168
  75.4 20.5 %attend.1 = (bf16[1024,1024]{1,0:T(8,128)(2,1)}, bf16[2048,128]{1,0:T(8,128)(2,1)}, bf16[2048,128]{1,0:T(8,128)(2,1)}, f32[1024,128]{1,0:T(8,128)}, f32[1024,128]{1,0:T(8,128)}) custom-call(s32[8,3072]{1,0:T(8,128)} %get-tuple-element.14.seg, f32[16,1024]{1,0:T(8,128)} %get-tuple-element.15.stats, bf16[1024,1024]{1,0:T(8,128)(2,1)} %get-tuple-element.16.q, ...), custom_call_target="tpu_custom_call" | custom-call | tf_op jit(solution)/shard_map/attend/pallas_call | solution.py:285
  95.9 64.1 %scatter_plane.1 = (bf16[128,8192]{1,0:T(8,128)(2,1)}, bf16[128,1024]{1,0:T(8,128)(2,1)}, bf16[128,1024]{1,0:T(8,128)(2,1)}) custom-call(bf16[1024,1024]{1,0:T(8,128)(2,1)} %get-tuple-element.20.dq, bf16[2048,128]{1,0:T(8,128)(2,1)} %get-tuple-element.21.dk_halo, bf16[2048,128]{1,0:T(8,128)(2,1)} %get-tuple-element.22.dv_halo, ...), custom_call_target="tpu_custom_call" | custom-call | tf_op jit(solution)/shard_map/scatter_plane/pallas_call | solution.py:390
  160.0 0.0 copy-start.1
  160.0 0.0 copy-start
  160.0 3.2 %copy.13 = bf16[128,8192]{1,0:T(8,128)(2,1)} copy(bf16[128,8192]{1,0:T(8,128)(2,1)} %get-tuple-element.28) | data formatting | bytes 4194304
  163.2 0.0 copy-done.1
  163.2 0.7 copy.14
  163.9 0.0 copy-done
  163.9 0.7 copy.15
Async XLA Ops:
  160.0 3.2 %copy-start.1 = (bf16[128,1024]{1,0:T(8,128)(2,1)S(1)}, bf16[128,1024]{1,0:T(8,128)(2,1)}, u32[]{:S(2)}) copy-start(bf16[128,1024]{1,0:T(8,128)(2,1)} %get-tuple-element.29) | copy-start | bytes 786436
  160.0 3.9 %copy-start = (bf16[128,1024]{1,0:T(8,128)(2,1)S(1)}, bf16[128,1024]{1,0:T(8,128)(2,1)}, u32[]{:S(2)}) copy-start(bf16[128,1024]{1,0:T(8,128)(2,1)} %get-tuple-element.30) | copy-start | bytes 786436

commit v3 on v2

--- a/solution.py
+++ b/solution.py
@@ -12,7 +12,10 @@
 LOG2E = math.log2(math.e)
 MESH = pl.DeviceIdType.MESH
 PLANE = 8
+PLANE_X = 4
 HALO = 2
+CHUNKS = 2
+ROUTE_SEMS = 10
 BLOCK = 256
 VMEM_LIMIT = 60 * 1024 * 1024
 
@@ -43,9 +46,70 @@
     pl.semaphore_wait(barrier, count)
 
 
+class Route:
+    def __init__(self, x_first, plane, rank, source, target, stage, sems):
+        self.x_first, self.plane = x_first, plane
+        self.y, self.x = rank // PLANE_X, lax.rem(rank, PLANE_X)
+        self.source, self.target, self.stage = source, target, stage
+        self.send, self.recv = sems
+
+    def rank(self, dy, dx):
+        y = self.y if dy == 0 else 1 - self.y
+        return y * PLANE_X + lax.rem(self.x + dx + PLANE_X, PLANE_X)
+
+    def copy(self, n, source, target, peer):
+        return pltpu.make_async_remote_copy(
+            source, target, self.send.at[n], self.recv.at[n],
+            device_id=dev(self.plane * PLANE + peer), device_id_type=MESH,
+        )
+
+    def first_leg(self, dx):
+        peer = self.rank(0, dx) if self.x_first else self.rank(1, 0)
+        return self.copy(dx - 1, self.source(self.rank(1, dx)), self.stage.at[dx - 1], peer)
+
+    def second_leg(self, dx):
+        if self.x_first:
+            origin, peer = self.rank(0, -dx), self.rank(1, 0)
+        else:
+            origin, peer = self.rank(1, 0), self.rank(0, dx)
+        return self.copy(2 + dx, self.stage.at[dx - 1], self.target(origin), peer)
+
+    def straight(self, dx):
+        peer = self.rank(0, dx) if dx else self.rank(1, 0)
+        return self.copy(6 + dx, self.source(peer), self.target(self.rank(0, 0)), peer)
+
+    def start_first(self):
+        for dx in range(1, PLANE_X):
+            self.first_leg(dx).start()
+
+    def start_straight(self):
+        for dx in range(PLANE_X):
+            self.straight(dx).start()
+
+    def pass_on(self):
+        for dx in range(1, PLANE_X):
+            self.first_leg(dx).wait_recv()
+            self.second_leg(dx).start()
+
+    def wait_arrivals(self):
+        for dx in range(PLANE_X):
+            origin = self.rank(0, -dx) if dx else self.rank(1, 0)
+            self.copy(6 + dx, self.target(origin), self.target(origin), origin).wait_recv()
+        for dx in range(1, PLANE_X):
+            origin = self.rank(1, -dx)
+            self.copy(2 + dx, self.target(origin), self.target(origin), origin).wait_recv()
+
+    def wait_sends(self):
+        for dx in range(1, PLANE_X):
+            self.first_leg(dx).wait_send()
+            self.second_leg(dx).wait_send()
+        for dx in range(PLANE_X):
+            self.straight(dx).wait_send()
+
+
 def gather_kernel(
     planes, q, g, o, k, v, seg, lse, q_all, g_all, k_win, v_win, stats_all, seg_win,
-    o_here, g_here, stats, seg_here, send, recv, z_send, z_recv, local,
+    o_here, g_here, stats, seg_here, stage, r_send, r_recv, send, recv, z_send, z_recv, local,
 ):
     rows = q.shape[0]
     span = rows * PLANE
@@ -65,11 +129,27 @@
         (lambda p: seg_here, lambda s: seg_win.at[:, own_part(s)]),
         (lambda p: k.at[:, part(p, D)], lambda s: k_win.at[own_part(s), :]),
         (lambda p: v.at[:, part(p, D)], lambda s: v_win.at[own_part(s), :]),
+        (lambda p: stats.at[part(p, 2 * heads), :], lambda s: stats_all.at[:, part(s, rows)]),
         (lambda p: q.at[:, part(p, wide)], lambda s: q_all.at[part(s, rows), :]),
         (lambda p: g.at[:, part(p, wide)], lambda s: g_all.at[part(s, rows), :]),
-        (lambda p: stats.at[part(p, 2 * heads), :], lambda s: stats_all.at[:, part(s, rows)]),
     ]
-    last = len(pieces) - 1
+    last = 3
+    narrow = wide // CHUNKS
+
+    def route(n, c):
+        array, gathered = ((q, q_all), (g, g_all))[n]
+
+        def source(p):
+            return array.at[:, pl.ds(pl.multiple_of(p * wide + c * narrow, narrow), narrow)]
+
+        def target(s):
+            return gathered.at[part(s, rows), pl.ds(c * narrow, narrow)]
+
+        return Route(
+            n == 0, plane, rank, source, target, stage.at[n, c], (r_send.at[n, c], r_recv.at[n, c])
+        )
+
+    routes = [route(n, c) for c in range(CHUNKS) for n in range(2)]
 
     def own_copy(n):
         source, target = pieces[n]
@@ -104,8 +184,8 @@
             device_id=dev(me + dz * PLANE), device_id_type=MESH,
         )
 
-    load_o = pltpu.make_async_copy(o, o_here, local.at[last + 1])
-    load_g = pltpu.make_async_copy(g, g_here, local.at[last + 2])
+    load_o = pltpu.make_async_copy(o, o_here, local.at[6])
+    load_g = pltpu.make_async_copy(g, g_here, local.at[7])
     load_o.start()
     load_g.start()
     seg_here[...] = jnp.broadcast_to(seg[...], seg_here.shape)
@@ -114,6 +194,12 @@
         for o_at in range(1, PLANE):
             plane_copy(n, o_at).start()
         own_copy(n).start()
+    for path in routes:
+        path.start_first()
+    for path in routes:
+        path.start_straight()
+    own_copy(4).start()
+    own_copy(5).start()
 
     load_o.wait()
     load_g.wait()
@@ -140,10 +226,16 @@
             @pl.when(plane + dz < planes)
             def _():
                 z_copy(n, dz).start()
-    for n in range(3, last + 1):
-        own_copy(n).wait()
-        for o_at in range(1, PLANE):
-            arrival(n, o_at).wait_recv()
+    for path in routes:
+        path.pass_on()
+    own_copy(last).wait()
+    own_copy(4).wait()
+    own_copy(5).wait()
+    for o_at in range(1, PLANE):
+        arrival(last, o_at).wait_recv()
+    for path in routes:
+        path.wait_arrivals()
+        path.wait_sends()
     for n in range(last + 1):
         for o_at in range(1, PLANE):
             plane_copy(n, o_at).wait_send()
@@ -182,8 +274,11 @@
             pltpu.VMEM(g.shape, g.dtype),
             pltpu.VMEM((2 * heads * PLANE, rows), jnp.float32),
             pltpu.VMEM((8, rows), jnp.int32),
-            pltpu.SemaphoreType.DMA((6, PLANE - 1)),
-            pltpu.SemaphoreType.DMA((6, PLANE - 1)),
+            pltpu.VMEM((2, CHUNKS, PLANE_X - 1, rows, heads * D // CHUNKS), q.dtype),
+            pltpu.SemaphoreType.DMA((2, CHUNKS, ROUTE_SEMS)),
+            pltpu.SemaphoreType.DMA((2, CHUNKS, ROUTE_SEMS)),
+            pltpu.SemaphoreType.DMA((4, PLANE - 1)),
+            pltpu.SemaphoreType.DMA((4, PLANE - 1)),
             pltpu.SemaphoreType.DMA((3, HALO)),
             pltpu.SemaphoreType.DMA((3, HALO)),
             pltpu.SemaphoreType.DMA((8,)),
@@ -310,7 +405,7 @@
 
 def scatter_kernel(
     planes, dq, dk_halo, dv_halo, dk_own, dv_own, grad_q, grad_k, grad_v,
-    dk_in, dv_in, dk_low, dv_low, total, send, recv, z_send, z_recv, last_send, last_recv, local,
+    dk_in, dv_in, dk_low, dv_low, total, stage, r_send, r_recv, z_send, z_recv, last_send, last_recv, local,
 ):
     rows = grad_q.shape[0]
     span = rows * PLANE
@@ -329,12 +424,18 @@
             device_id=dev(me - dz * PLANE), device_id_type=MESH,
         )
 
-    def q_copy(o, origin):
-        peer = lax.rem(rank + o, PLANE)
-        return pltpu.make_async_remote_copy(
-            dq.at[cols(peer, rows), :], grad_q.at[:, cols(origin, wide)], send.at[o - 1], recv.at[o - 1],
-            device_id=dev(plane * PLANE + peer), device_id_type=MESH,
-        )
+    def route(c):
+        narrow = wide // 2
+
+        def source(p):
+            return dq.at[cols(p, rows), pl.ds(c * narrow, narrow)]
+
+        def target(s):
+            return grad_q.at[:, pl.ds(pl.multiple_of(s * wide + c * narrow, narrow), narrow)]
+
+        return Route(c == 0, plane, rank, source, target, stage.at[c], (r_send.at[c], r_recv.at[c]))
+
+    routes = [route(c) for c in range(2)]
 
     def kv_copy(n, o, origin):
         low, out = ((dk_low, grad_k), (dv_low, grad_v))[n]
@@ -350,10 +451,14 @@
             @pl.when(plane >= dz)
             def _():
                 z_copy(n, dz).start()
-    for o in range(1, PLANE):
-        q_copy(o, rank).start()
+    for path in routes:
+        path.start_first()
+    for path in routes:
+        path.start_straight()
     own_q = pltpu.make_async_copy(dq.at[cols(rank, rows), :], grad_q.at[:, cols(rank, wide)], local.at[0])
     own_q.start()
+    for path in routes:
+        path.pass_on()
     own_kv = []
     for n in range(2):
         low, out, own, into = ((dk_low, grad_k, dk_own, dk_in), (dv_low, grad_v, dv_own, dv_in))[n]
@@ -375,9 +480,11 @@
             @pl.when(plane >= dz)
             def _():
                 z_copy(n, dz).wait_send()
+    for path in routes:
+        path.wait_arrivals()
+        path.wait_sends()
     for o in range(1, PLANE):
         origin = lax.rem(rank + PLANE - o, PLANE)
-        q_copy(o, origin).wait()
         for n in range(2):
             kv_copy(n, o, origin).wait()
 
@@ -402,8 +509,9 @@
             pltpu.VMEM((span, D), jnp.bfloat16),
             pltpu.VMEM((span, D), jnp.bfloat16),
             pltpu.VMEM((span, D), jnp.float32),
-            pltpu.SemaphoreType.DMA((PLANE - 1,)),
-            pltpu.SemaphoreType.DMA((PLANE - 1,)),
+            pltpu.VMEM((2, PLANE_X - 1, rows, wide // 2), dq.dtype),
+            pltpu.SemaphoreType.DMA((2, ROUTE_SEMS)),
+            pltpu.SemaphoreType.DMA((2, ROUTE_SEMS)),
             pltpu.SemaphoreType.DMA((2, HALO)),
             pltpu.SemaphoreType.DMA((2, HALO)),
             pltpu.SemaphoreType.DMA((2, PLANE - 1)),

time: 167 us -> 158 us (0.946)
  the two profiles are of different devices: /device:TPU:96 before, /device:TPU:16 now
where the time goes in v3:
time: 158 us
  Pallas kernels  153 us (97%)
  local copies, waits for them, and re-layouts  4.56 us (3%)
    pallas_call x1, Pallas kernels, scatter(): pl.pallas_call(functools.partial(scatter_kernel, planes), out_shape=(jax....  68 us
    pallas_call x1, Pallas kernels, gather(): pl.pallas_call(functools.partial(gather_kernel, planes), out_shape=(jax.S...  60.8 us
    pallas_call x1, Pallas kernels, attend(): pl.pallas_call(attend_kernel, grid=(span // BLOCK,), in_specs=[whole(seg_...  23.6 us
    unnamed x7, local copies, waits for them, and re-layouts  4.56 us

profile of v3, /device:TPU:16, one launch (start us, length us, event | category | flops | bytes accessed | tf_op | source)
XLA Modules:
  0.0 157.8 jit_solution(12034800159490919282)
XLA Ops:
  0.6 60.8 %gather_plane.1 = (bf16[1024,1024]{1,0:T(8,128)(2,1)}, bf16[1024,1024]{1,0:T(8,128)(2,1)}, bf16[3072,128]{1,0:T(8,128)(2,1)}, bf16[3072,128]{1,0:T(8,128)(2,1)}, f32[16,1024]{1,0:T(8,128)}, /*index=5*/s32[8,3072]{1,0:T(8,128)}) custom-call(bf16[128,8192]{1,0:T(8,128)(2,1)} %q.1, bf16[128,8192]{1,0:T(8,128)(2,1)} %g.1, bf16[128,8192]{1,0:T(8,128)(2,1)} %o.1, ...), custom_call_target="tpu_custom_call" | custom-call | tf_op jit(solution)/shard_map/gather_plane/pallas_call | solution.py:260
  61.5 23.6 %attend.1 = (bf16[1024,1024]{1,0:T(8,128)(2,1)}, bf16[2048,128]{1,0:T(8,128)(2,1)}, bf16[2048,128]{1,0:T(8,128)(2,1)}, f32[1024,128]{1,0:T(8,128)}, f32[1024,128]{1,0:T(8,128)}) custom-call(s32[8,3072]{1,0:T(8,128)} %get-tuple-element.14.seg, f32[16,1024]{1,0:T(8,128)} %get-tuple-element.15.stats, bf16[1024,1024]{1,0:T(8,128)(2,1)} %get-tuple-element.16.q, ...), custom_call_target="tpu_custom_call" | custom-call | tf_op jit(solution)/shard_map/attend/pallas_call | solution.py:380
  85.1 68.0 %scatter_plane.1 = (bf16[128,8192]{1,0:T(8,128)(2,1)}, bf16[128,1024]{1,0:T(8,128)(2,1)}, bf16[128,1024]{1,0:T(8,128)(2,1)}) custom-call(bf16[1024,1024]{1,0:T(8,128)(2,1)} %get-tuple-element.20.dq, bf16[2048,128]{1,0:T(8,128)(2,1)} %get-tuple-element.21.dk_halo, bf16[2048,128]{1,0:T(8,128)(2,1)} %get-tuple-element.22.dv_halo, ...), custom_call_target="tpu_custom_call" | custom-call | tf_op jit(solution)/shard_map/scatter_plane/pallas_call | solution.py:497
  153.2 0.0 copy-start.1
  153.2 0.0 copy-start
  153.2 3.2 %copy.13 = bf16[128,8192]{1,0:T(8,128)(2,1)} copy(bf16[128,8192]{1,0:T(8,128)(2,1)} %get-tuple-element.28) | data formatting | bytes 4194304
  156.3 0.0 copy-done.1
  156.3 0.7 copy.14
  157.1 0.0 copy-done
  157.1 0.7 copy.15
Async XLA Ops:
  153.2 3.2 %copy-start.1 = (bf16[128,1024]{1,0:T(8,128)(2,1)S(1)}, bf16[128,1024]{1,0:T(8,128)(2,1)}, u32[]{:S(2)}) copy-start(bf16[128,1024]{1,0:T(8,128)(2,1)} %get-tuple-element.29) | copy-start | bytes 786436
  153.2 3.9 %copy-start = (bf16[128,1024]{1,0:T(8,128)(2,1)S(1)}, bf16[128,1024]{1,0:T(8,128)(2,1)}, u32[]{:S(2)}) copy-start(bf16[128,1024]{1,0:T(8,128)(2,1)} %get-tuple-element.30) | copy-start | bytes 786436

commit v4 on v3

v4 whole, which is shorter than its diff:
```python
import functools
import math

import jax
import jax.numpy as jnp
from jax import lax
from jax.experimental import pallas as pl
from jax.experimental.pallas import tpu as pltpu
from jax.sharding import PartitionSpec as P

D = 128
LOG2E = math.log2(math.e)
MESH = pl.DeviceIdType.MESH
PLANE = 8
PLANE_X = 4
HALO = 2
NEAR = 2
CHUNKS = 4
ROUTE_SEMS = 10
BLOCK = 256
VMEM_LIMIT = 60 * 1024 * 1024


def dev(index):
    return {"seq": index}


def greet(me, plane, rank, planes, reach):
    barrier = pltpu.get_barrier_semaphore()
    for o in range(1, PLANE):
        peer = plane * PLANE + lax.rem(rank + o, PLANE)
        pl.semaphore_signal(barrier, inc=1, device_id=dev(peer), device_id_type=MESH)
    count = PLANE - 1
    for dz in range(1, reach + 1):
        up = plane + dz < planes
        down = plane >= dz

        @pl.when(up)
        def _():
            pl.semaphore_signal(barrier, inc=1, device_id=dev(me + dz * PLANE), device_id_type=MESH)

        @pl.when(down)
        def _():
            pl.semaphore_signal(barrier, inc=1, device_id=dev(me - dz * PLANE), device_id_type=MESH)

        count = count + up.astype(jnp.int32) + down.astype(jnp.int32)
    pl.semaphore_wait(barrier, count)


class Route:
    def __init__(self, x_first, plane, rank, source, target, stage, sems):
        self.x_first, self.plane = x_first, plane
        self.y, self.x = rank // PLANE_X, lax.rem(rank, PLANE_X)
        self.source, self.target, self.stage = source, target, stage
        self.send, self.recv = sems

    def rank(self, dy, dx):
        y = self.y if dy == 0 else 1 - self.y
        return y * PLANE_X + lax.rem(self.x + dx + PLANE_X, PLANE_X)

    def copy(self, n, source, target, peer):
        return pltpu.make_async_remote_copy(
            source, target, self.send.at[n], self.recv.at[n],
            device_id=dev(self.plane * PLANE + peer), device_id_type=MESH,
        )

    def first_leg(self, dx):
        peer = self.rank(0, dx) if self.x_first else self.rank(1, 0)
        return self.copy(dx - 1, self.source(self.rank(1, dx)), self.stage.at[dx - 1], peer)

    def second_leg(self, dx):
        if self.x_first:
            origin, peer = self.rank(0, -dx), self.rank(1, 0)
        else:
            origin, peer = self.rank(1, 0), self.rank(0, dx)
        return self.copy(2 + dx, self.stage.at[dx - 1], self.target(origin), peer)

    def straight(self, dx):
        peer = self.rank(0, dx) if dx else self.rank(1, 0)
        return self.copy(6 + dx, self.source(peer), self.target(self.rank(0, 0)), peer)

    def start_first(self):
        for dx in range(1, PLANE_X):
            self.first_leg(dx).start()

    def start_straight(self):
        for dx in range(PLANE_X):
            self.straight(dx).start()

    def pass_on(self):
        for dx in range(1, PLANE_X):
            self.first_leg(dx).wait_recv()
            self.second_leg(dx).start()

    def wait_arrivals(self):
        for dx in range(PLANE_X):
            origin = self.rank(0, -dx) if dx else self.rank(1, 0)
            self.copy(6 + dx, self.target(origin), self.target(origin), origin).wait_recv()
        for dx in range(1, PLANE_X):
            origin = self.rank(1, -dx)
            self.copy(2 + dx, self.target(origin), self.target(origin), origin).wait_recv()

    def wait_sends(self):
        for dx in range(1, PLANE_X):
            self.first_leg(dx).wait_send()
            self.second_leg(dx).wait_send()
        for dx in range(PLANE_X):
            self.straight(dx).wait_send()


def tile_terms(k_rows, v_rows, q_rows, g_rows, lse_row, delta_row, visible):
    nt = (((1,), (1,)), ((), ()))
    scores = lax.dot_general(k_rows, q_rows, nt, preferred_element_type=jnp.float32)
    weights = jnp.exp2(scores * (LOG2E / math.sqrt(D)) - lse_row)
    if visible is not None:
        weights = jnp.where(visible(), weights, 0.0)
    d_weights = lax.dot_general(v_rows, g_rows, nt, preferred_element_type=jnp.float32)
    dscore = (weights * (d_weights - delta_row)).astype(jnp.bfloat16)
    return weights.astype(jnp.bfloat16), dscore


def begins_at(ids, first):
    at = lax.broadcasted_iota(jnp.int32, ids.shape, 1)
    begins = (ids != pltpu.roll(ids, 1, 1)) & (at > first)
    found = jnp.where(begins, at, first)
    step = 1
    while step < ids.shape[1]:
        found = jnp.where(at >= step, jnp.maximum(found, pltpu.roll(found, step, 1)), found)
        step *= 2
    return found


def gather_kernel(
    planes, q, g, o, k, v, seg, lse, q_all, g_all, k_win, v_win, dq_part, stats_all, seg_win, dk, dv,
    o_here, g_here, q_in, g_in, k_in, v_in, k_t, start, dq_t, stats, seg_here, stage,
    r_send, r_recv, send, recv, z_send, z_recv, local, chunk_out,
):
    rows = q.shape[0]
    span = rows * PLANE
    wide = q_in.shape[1]
    heads = wide // D
    me = lax.axis_index("seq")
    plane, rank = me // PLANE, lax.rem(me, PLANE)
    own = HALO * span
    narrow = wide // CHUNKS
    per_chunk = narrow // D
    across = per_chunk * BLOCK
    near = NEAR * BLOCK

    def part(index, width):
        return pl.ds(pl.multiple_of(index * width, width), width)

    def own_part(s):
        return pl.ds(pl.multiple_of(own + s * rows, rows), rows)

    pieces = [
        (lambda p: seg_here, lambda s: seg_win.at[:, own_part(s)]),
        (lambda p: k.at[:, part(p, D)], lambda s: k_win.at[own_part(s), :]),
        (lambda p: v.at[:, part(p, D)], lambda s: v_win.at[own_part(s), :]),
        (lambda p: stats.at[part(p, 2 * heads), :], lambda s: stats_all.at[:, part(s, rows)]),
        (lambda p: q.at[:, part(p, wide)], lambda s: q_in.at[part(s, rows), :]),
        (lambda p: g.at[:, part(p, wide)], lambda s: g_in.at[part(s, rows), :]),
    ]
    last = 3

    def routes(c):
        made = []
        for n, (array, gathered) in enumerate(((q, q_in), (g, g_in))):
            def source(p, array=array):
                return array.at[:, pl.ds(pl.multiple_of(p * wide + c * narrow, narrow), narrow)]

            def target(s, gathered=gathered):
                return gathered.at[part(s, rows), part(c, narrow)]

            made.append(Route(
                n == 0, plane, rank, source, target, stage.at[n, c], (r_send.at[n, c], r_recv.at[n, c])
            ))
        return made

    def own_copy(n):
        source, target = pieces[n]
        return pltpu.make_async_copy(source(rank), target(rank), local.at[n])

    def plane_copy(n, o):
        source, target = pieces[n]
        peer = lax.rem(rank + o, PLANE)
        return pltpu.make_async_remote_copy(
            source(peer), target(rank), send.at[n, o - 1], recv.at[n, o - 1],
            device_id=dev(plane * PLANE + peer), device_id_type=MESH,
        )

    def arrival(n, o):
        source, target = pieces[n]
        origin = lax.rem(rank + PLANE - o, PLANE)
        return pltpu.make_async_remote_copy(
            source(rank), target(origin), send.at[n, o - 1], recv.at[n, o - 1],
            device_id=dev(plane * PLANE + origin), device_id_type=MESH,
        )

    def z_copy(n, dz):
        held, there = pl.ds(own - (dz - 1) * span, span), pl.ds(own - dz * span, span)
        if n == 0:
            source, target = seg_win.at[:, held], seg_win.at[:, there]
        else:
            win = (k_win, v_win)[n - 1]
            source, target = win.at[held, :], win.at[there, :]
        return pltpu.make_async_remote_copy(
            source, target, z_send.at[n, dz - 1], z_recv.at[n, dz - 1],
            device_id=dev(me + PLANE), device_id_type=MESH,
        )

    def z_sends(dz):
        return (plane + 1 < planes) & (plane + 1 >= dz)

    def start_chunk(c):
        for path in routes(c):
            path.start_first()
        for path in routes(c):
            path.start_straight()

    def pass_on(c):
        for path in routes(c):
            path.pass_on()

    def put_copy(n, c):
        here = part(c, narrow)
        if n == 0:
            return pltpu.make_async_copy(q_in.at[:, here], q_all.at[:, here], chunk_out.at[n, c])
        if n == 1:
            return pltpu.make_async_copy(g_in.at[:, here], g_all.at[:, here], chunk_out.at[n, c])
        here = part(c, across)
        return pltpu.make_async_copy(dq_t.at[:, here], dq_part.at[:, here], chunk_out.at[n, c])

    load_o = pltpu.make_async_copy(o, o_here, local.at[6])
    load_g = pltpu.make_async_copy(g, g_here, local.at[7])
    load_o.start()
    load_g.start()
    seg_here[...] = jnp.broadcast_to(seg[...], seg_here.shape)
    greet(me, plane, rank, planes, 1)
    for n in range(last):
        for o_at in range(1, PLANE):
            plane_copy(n, o_at).start()
        own_copy(n).start()
    start_chunk(0)
    start_chunk(1)
    own_copy(4).start()
    own_copy(5).start()

    load_o.wait()
    load_g.wait()

    @pl.loop(0, PLANE)
    def _(p):
        sums = []
        for h in range(heads):
            features = pl.ds(pl.multiple_of(p * wide + h * D, D), D)
            product = o_here[:, features].astype(jnp.float32) * g_here[:, features].astype(jnp.float32)
            sums.append(jnp.sum(product.T, axis=0, keepdims=True))
        stats[part(p * 2, heads), :] = lse[part(p, heads), :]
        stats[part(p * 2 + 1, heads), :] = jnp.concatenate(sums, axis=0)

    for o_at in range(1, PLANE):
        plane_copy(last, o_at).start()
    own_copy(last).start()

    for n in range(3):
        own_copy(n).wait()
        for o_at in range(1, PLANE):
            arrival(n, o_at).wait_recv()
        @pl.when(z_sends(1))
        def _():
            z_copy(n, 1).start()

    load_k = pltpu.make_async_copy(k_win.at[pl.ds(own, span), :], k_in.at[pl.ds(near, span), :], local.at[6])
    load_v = pltpu.make_async_copy(v_win.at[pl.ds(own, span), :], v_in.at[pl.ds(near, span), :], local.at[7])
    load_k.start()
    load_v.start()
    pass_on(0)
    dk[...] = jnp.zeros_like(dk)
    dv[...] = jnp.zeros_like(dv)
    load_k.wait()
    load_v.wait()
    for n in range(3):
        @pl.when(plane >= 1)
        def _():
            z_copy(n, 1).wait_recv()

        @pl.when(z_sends(2))
        def _():
            z_copy(n, 2).start()

    load_k = pltpu.make_async_copy(k_win.at[pl.ds(own - near, near), :], k_in.at[pl.ds(0, near), :], local.at[6])
    load_v = pltpu.make_async_copy(v_win.at[pl.ds(own - near, near), :], v_in.at[pl.ds(0, near), :], local.at[7])

    @pl.when(plane >= 1)
    def _():
        load_k.start()
        load_v.start()
        load_k.wait()
        load_v.wait()

    @pl.when(plane < 1)
    def _():
        k_in[:near, :] = jnp.zeros((near, D), k_in.dtype)
        v_in[:near, :] = jnp.zeros((near, D), v_in.dtype)

    known = jnp.where(plane >= 1, 0, near)
    start[...] = begins_at(seg_win[:, pl.ds(own - near, near + span)], known)[:, near:]
    k_t[...] = k_in[...].T
    own_copy(last).wait()
    own_copy(4).wait()
    own_copy(5).wait()
    for o_at in range(1, PLANE):
        arrival(last, o_at).wait_recv()

    @pl.loop(0, CHUNKS)
    def _(c):
        @pl.when(c + 2 < CHUNKS)
        def _():
            start_chunk(c + 2)

        @pl.when(c + 1 < CHUNKS)
        def _():
            pass_on(c + 1)

        for path in routes(c):
            path.wait_arrivals()
        put_copy(0, c).start()
        put_copy(1, c).start()

        blocks = span // BLOCK
        operands = []
        for i in range(blocks):
            here = pl.ds(i * BLOCK, BLOCK)

            def stacked(ref, here=here):
                return jnp.concatenate(
                    [ref[here, pl.ds(pl.multiple_of(c * narrow + h * D, D), D)] for h in range(per_chunk)], axis=0
                )

            def in_line(first, here=here):
                return jnp.concatenate(
                    [stats_all[pl.ds(first + c * per_chunk + h, 1), here] for h in range(per_chunk)], axis=1
                )

            start_row = jnp.concatenate([start[0:1, here]] * per_chunk, axis=1)
            operands.append((stacked(q_in), stacked(g_in), in_line(0) * LOG2E, in_line(heads), start_row))
        totals = [jnp.zeros((D, across), jnp.float32) for _ in range(blocks)]
        down = lax.broadcasted_iota(jnp.int32, (BLOCK, across), 0)
        query_at = lax.rem(lax.broadcasted_iota(jnp.int32, (1, across), 1), BLOCK)
        for back in range(blocks + NEAR):
            for i in range(blocks):
                j = NEAR + i - back
                if j < 0:
                    continue
                there = pl.ds(j * BLOCK, BLOCK)
                q_rows, g_rows, lse_row, delta_row, start_row = operands[i]

                def visible(j=j, back=back, start_row=start_row):
                    seen = down >= start_row - j * BLOCK
                    return seen & (down <= query_at) if back == 0 else seen

                low, dscore = tile_terms(k_in[there, :], v_in[there, :], q_rows, g_rows, lse_row, delta_row, visible)
                dv[there, :] += jnp.dot(low, g_rows, preferred_element_type=jnp.float32)
                dk[there, :] += jnp.dot(dscore, q_rows, preferred_element_type=jnp.float32)
                totals[i] += jnp.dot(k_t[:, there], dscore, preferred_element_type=jnp.float32)
        for i in range(blocks):
            dq_t[pl.ds(i * D, D), part(c, across)] = totals[i]

        put_copy(2, c).start()

    for c in range(CHUNKS):
        for path in routes(c):
            path.wait_sends()
        for n in range(3):
            put_copy(n, c).wait()
    for n in range(last + 1):
        for o_at in range(1, PLANE):
            plane_copy(n, o_at).wait_send()
    for n in range(3):
        for dz in range(1, HALO + 1):
            @pl.when(z_sends(dz))
            def _():
                z_copy(n, dz).wait_send()

        @pl.when(plane >= 2)
        def _():
            z_copy(n, 2).wait_recv()


def gather(q, g, o, k, v, seg, lse, planes):
    rows = q.shape[0]
    span = rows * PLANE
    heads = lse.shape[0] // PLANE
    wide = heads * D
    window = (HALO + 1) * span
    near = NEAR * BLOCK
    part_shape = (span // BLOCK * D, heads * BLOCK)
    any_space = pl.BlockSpec(memory_space=pl.ANY)
    vmem = pl.BlockSpec(memory_space=pltpu.VMEM)
    return pl.pallas_call(
        functools.partial(gather_kernel, planes),
        out_shape=(
            jax.ShapeDtypeStruct((span, wide), q.dtype),
            jax.ShapeDtypeStruct((span, wide), g.dtype),
            jax.ShapeDtypeStruct((window, D), k.dtype),
            jax.ShapeDtypeStruct((window, D), v.dtype),
            jax.ShapeDtypeStruct(part_shape, jnp.float32),
            jax.ShapeDtypeStruct((2 * heads, span), lse.dtype),
            jax.ShapeDtypeStruct((8, window), seg.dtype),
            jax.ShapeDtypeStruct((near + span, D), jnp.float32),
            jax.ShapeDtypeStruct((near + span, D), jnp.float32),
        ),
        in_specs=[any_space] * 5 + [vmem] * 2,
        out_specs=(any_space,) * 5 + (vmem,) * 4,
        scratch_shapes=[
            pltpu.VMEM(o.shape, o.dtype),
            pltpu.VMEM(g.shape, g.dtype),
            pltpu.VMEM((span, wide), q.dtype),
            pltpu.VMEM((span, wide), g.dtype),
            pltpu.VMEM((near + span, D), k.dtype),
            pltpu.VMEM((near + span, D), v.dtype),
            pltpu.VMEM((D, near + span), k.dtype),
            pltpu.VMEM((8, span), jnp.int32),
            pltpu.VMEM(part_shape, jnp.float32),
            pltpu.VMEM((2 * heads * PLANE, rows), jnp.float32),
            pltpu.VMEM((8, rows), jnp.int32),
            pltpu.VMEM((2, CHUNKS, PLANE_X - 1, rows, wide // CHUNKS), q.dtype),
            pltpu.SemaphoreType.DMA((2, CHUNKS, ROUTE_SEMS)),
            pltpu.SemaphoreType.DMA((2, CHUNKS, ROUTE_SEMS)),
            pltpu.SemaphoreType.DMA((4, PLANE - 1)),
            pltpu.SemaphoreType.DMA((4, PLANE - 1)),
            pltpu.SemaphoreType.DMA((3, HALO)),
            pltpu.SemaphoreType.DMA((3, HALO)),
            pltpu.SemaphoreType.DMA((8,)),
            pltpu.SemaphoreType.DMA((3, CHUNKS)),
        ],
        compiler_params=pltpu.CompilerParams(
            collective_id=0, has_side_effects=True, vmem_limit_bytes=VMEM_LIMIT
        ),
        name="gather_plane",
    )(q, g, o, k, v, seg, lse)


def attend_kernel(seg, stats, q, g, k, v, dq_part, dk_near, dv_near, dq, dk_halo, dv_halo, dk, dv, k_t, start):
    i = pl.program_id(0)
    own = k.shape[0]
    span = own // HALO
    heads = q.shape[1] // D
    across = heads * BLOCK
    inv_root = 1.0 / math.sqrt(D)
    halo_end = own // BLOCK - NEAR

    @pl.when(i == 0)
    def _():
        far = halo_end * BLOCK
        dk[:far, :] = jnp.zeros((far, D), jnp.float32)
        dv[:far, :] = jnp.zeros((far, D), jnp.float32)
        dk[far:, :] = dk_near[...]
        dv[far:, :] = dv_near[...]
        k_t[...] = k[...].T
        plane = lax.axis_index("seq") // PLANE
        found = begins_at(seg[...], own - jnp.minimum(plane, HALO) * span)
        start[...] = found[:, own:]

    block_start = start[0:1, pl.ds(pl.multiple_of(i * BLOCK, BLOCK), BLOCK)]
    position = block_start.astype(jnp.float32)
    low_end = jnp.minimum(jnp.min(position).astype(jnp.int32) // BLOCK, halo_end)
    full = (jnp.max(position).astype(jnp.int32) + BLOCK - 1) // BLOCK
    full = jnp.clip(full, low_end, halo_end)

    def put(total):
        for h in range(heads):
            dq[:, h * D:(h + 1) * D] = (total[:, h * BLOCK:(h + 1) * BLOCK].T * inv_root).astype(dq.dtype)

    @pl.when(low_end == halo_end)
    def _():
        put(dq_part)

    @pl.when(low_end < halo_end)
    def _():
        def stacked(ref):
            return jnp.concatenate([ref[:, h * D:(h + 1) * D] for h in range(heads)], axis=0)

        def in_line(first):
            return jnp.concatenate([stats[first + h:first + h + 1, :] for h in range(heads)], axis=1)

        q_rows, g_rows = stacked(q), stacked(g)
        lse_row = in_line(0) * LOG2E
        delta_row = in_line(heads)
        start_row = jnp.concatenate([block_start] * heads, axis=1)

        def tile(masked, j, total):
            there = pl.ds(pl.multiple_of(j * BLOCK, BLOCK), BLOCK)

            def visible():
                return j * BLOCK + lax.broadcasted_iota(jnp.int32, (BLOCK, across), 0) >= start_row

            low, dscore = tile_terms(
                k[there, :], v[there, :], q_rows, g_rows, lse_row, delta_row, visible if masked else None
            )
            dv[there, :] += jnp.dot(low, g_rows, preferred_element_type=jnp.float32)
            dk[there, :] += jnp.dot(dscore, q_rows, preferred_element_type=jnp.float32)
            return total + jnp.dot(k_t[:, there], dscore, preferred_element_type=jnp.float32)

        total = lax.fori_loop(low_end, full, functools.partial(tile, True), dq_part[...])
        put(lax.fori_loop(full, halo_end, functools.partial(tile, False), total))

    @pl.when(i == pl.num_programs(0) - 1)
    def _():
        dk_halo[...] = (dk[...] * inv_root).astype(dk_halo.dtype)
        dv_halo[...] = dv[...].astype(dv_halo.dtype)


def attend(q, g, k, v, dq_part, dk, dv, stats, seg_win):
    span, wide = q.shape
    window = k.shape[0]
    own = window - span
    near = NEAR * BLOCK
    block = pl.BlockSpec((BLOCK, wide), lambda i: (i, 0))

    def whole(shape):
        return pl.BlockSpec(shape, lambda i: (0, 0))

    return pl.pallas_call(
        attend_kernel,
        grid=(span // BLOCK,),
        in_specs=[
            whole(seg_win.shape), pl.BlockSpec((stats.shape[0], BLOCK), lambda i: (0, i)),
            block, block, whole((own, D)), whole((own, D)),
            pl.BlockSpec((D, dq_part.shape[1]), lambda i: (i, 0)), whole((near, D)), whole((near, D)),
        ],
        out_specs=[block, whole((own, D)), whole((own, D))],
        out_shape=(
            jax.ShapeDtypeStruct((span, wide), q.dtype),
            jax.ShapeDtypeStruct((own, D), jnp.bfloat16),
            jax.ShapeDtypeStruct((own, D), jnp.bfloat16),
        ),
        scratch_shapes=[
            pltpu.VMEM((own, D), jnp.float32),
            pltpu.VMEM((own, D), jnp.float32),
            pltpu.VMEM((D, own), jnp.bfloat16),
            pltpu.VMEM((8, span), jnp.int32),
        ],
        compiler_params=pltpu.CompilerParams(vmem_limit_bytes=VMEM_LIMIT),
        name="attend",
    )(seg_win, stats, q, g, k, v, dq_part, dk, dv)


def scatter_kernel(
    planes, dq, dk_halo, dv_halo, dk_own, dv_own, grad_q, grad_k, grad_v,
    dk_in, dv_in, dk_low, dv_low, total, stage, r_send, r_recv, z_send, z_recv, last_send, last_recv, local,
):
    rows = grad_q.shape[0]
    span = rows * PLANE
    wide = dq.shape[1]
    me = lax.axis_index("seq")
    plane, rank = me // PLANE, lax.rem(me, PLANE)

    def cols(index, width):
        return pl.ds(pl.multiple_of(index * width, width), width)

    def z_copy(n, dz):
        halo, into = ((dk_halo, dk_in), (dv_halo, dv_in))[n]
        return pltpu.make_async_remote_copy(
            halo.at[pl.ds((HALO - dz) * span, span), :], into.at[dz - 1],
            z_send.at[n, dz - 1], z_recv.at[n, dz - 1],
            device_id=dev(me - dz * PLANE), device_id_type=MESH,
        )

    def route(c):
        narrow = wide // CHUNKS

        def source(p):
            return dq.at[cols(p, rows), pl.ds(c * narrow, narrow)]

        def target(s):
            return grad_q.at[:, pl.ds(pl.multiple_of(s * wide + c * narrow, narrow), narrow)]

        return Route(c % 2 == 0, plane, rank, source, target, stage.at[c], (r_send.at[c], r_recv.at[c]))

    routes = [route(c) for c in range(CHUNKS)]

    def kv_copy(n, o, origin):
        low, out = ((dk_low, grad_k), (dv_low, grad_v))[n]
        peer = lax.rem(rank + o, PLANE)
        return pltpu.make_async_remote_copy(
            low.at[cols(peer, rows), :], out.at[:, cols(origin, D)], last_send.at[n, o - 1], last_recv.at[n, o - 1],
            device_id=dev(plane * PLANE + peer), device_id_type=MESH,
        )

    greet(me, plane, rank, planes, HALO)
    for n in range(2):
        for dz in range(1, HALO + 1):
            @pl.when(plane >= dz)
            def _():
                z_copy(n, dz).start()
    def begin(c):
        routes[c].start_first()
        routes[c].start_straight()

    begin(0)
    begin(1)
    own_q = pltpu.make_async_copy(dq.at[cols(rank, rows), :], grad_q.at[:, cols(rank, wide)], local.at[0])
    own_q.start()
    for c in range(CHUNKS):
        routes[c].pass_on()
        if c + 2 < CHUNKS:
            begin(c + 2)
    own_kv = []
    for n in range(2):
        low, out, own, into = ((dk_low, grad_k, dk_own, dk_in), (dv_low, grad_v, dv_own, dv_in))[n]
        total[...] = own[pl.ds(own.shape[0] - span, span), :] * (1.0 / math.sqrt(D) if n == 0 else 1.0)
        for dz in range(1, HALO + 1):
            @pl.when(plane + dz < planes)
            def _():
                z_copy(n, dz).wait_recv()
                total[...] += into[dz - 1].astype(jnp.float32)
        low[...] = total[...].astype(low.dtype)
        for o in range(1, PLANE):
            kv_copy(n, o, rank).start()
        own_kv.append(pltpu.make_async_copy(low.at[cols(rank, rows), :], out.at[:, cols(rank, D)], local.at[1 + n]))
        own_kv[n].start()
    own_q.wait()
    for n in range(2):
        own_kv[n].wait()
        for dz in range(1, HALO + 1):
            @pl.when(plane >= dz)
            def _():
                z_copy(n, dz).wait_send()
    for path in routes:
        path.wait_arrivals()
        path.wait_sends()
    for o in range(1, PLANE):
        origin = lax.rem(rank + PLANE - o, PLANE)
        for n in range(2):
            kv_copy(n, o, origin).wait()


def scatter(dq, dk_halo, dv_halo, dk_own, dv_own, planes):
    span, wide = dq.shape
    rows = span // PLANE
    any_space = pl.BlockSpec(memory_space=pl.ANY)
    vmem = pl.BlockSpec(memory_space=pltpu.VMEM)
    return pl.pallas_call(
        functools.partial(scatter_kernel, planes),
        out_shape=(
            jax.ShapeDtypeStruct((rows, PLANE * wide), dq.dtype),
            jax.ShapeDtypeStruct((rows, PLANE * D), jnp.bfloat16),
            jax.ShapeDtypeStruct((rows, PLANE * D), jnp.bfloat16),
        ),
        in_specs=[any_space] * 3 + [vmem] * 2,
        out_specs=(any_space,) * 3,
        scratch_shapes=[
            pltpu.VMEM((HALO, span, D), jnp.bfloat16),
            pltpu.VMEM((HALO, span, D), jnp.bfloat16),
            pltpu.VMEM((span, D), jnp.bfloat16),
            pltpu.VMEM((span, D), jnp.bfloat16),
            pltpu.VMEM((span, D), jnp.float32),
            pltpu.VMEM((CHUNKS, PLANE_X - 1, rows, wide // CHUNKS), dq.dtype),
            pltpu.SemaphoreType.DMA((CHUNKS, ROUTE_SEMS)),
            pltpu.SemaphoreType.DMA((CHUNKS, ROUTE_SEMS)),
            pltpu.SemaphoreType.DMA((2, HALO)),
            pltpu.SemaphoreType.DMA((2, HALO)),
            pltpu.SemaphoreType.DMA((2, PLANE - 1)),
            pltpu.SemaphoreType.DMA((2, PLANE - 1)),
            pltpu.SemaphoreType.DMA((3,)),
        ],
        compiler_params=pltpu.CompilerParams(
            collective_id=1, has_side_effects=True, vmem_limit_bytes=VMEM_LIMIT
        ),
        name="scatter_plane",
    )(dq, dk_halo, dv_halo, dk_own, dv_own)


def on_device(queries, keys, values, outputs, out_grad, lse, segments):
    planes = lax.axis_size("seq") // PLANE
    q, g, k, v, dq_part, stats, seg_win, dk, dv = gather(
        queries, out_grad, outputs, keys, values, segments[None, :], lse, planes
    )
    return scatter(*attend(q, g, k, v, dq_part, dk, dv, stats, seg_win), dk, dv, planes)


def solution(mesh):
    rows = P(("dp", "seq"), None)
    in_specs = (rows, rows, rows, rows, rows, P(None, ("dp", "seq")), P(("dp", "seq")))
    return jax.shard_map(
        on_device, mesh=mesh, in_specs=in_specs, out_specs=(rows, rows, rows), check_vma=False
    )
```

time: 158 us -> 150 us (0.949)
  the two profiles are of different devices: /device:TPU:16 before, /device:TPU:96 now
where the time goes in v4:
time: 150 us; the launch traced here: 148 us
  Pallas kernels  143 us (95%)
  local copies, waits for them, and re-layouts  4.56 us (3%)
    pallas_call x1, Pallas kernels, gather(): pl.pallas_call(functools.partial(gather_kernel, planes), out_shape=(jax.S...  75 us
    pallas_call x1, Pallas kernels, scatter(): pl.pallas_call(functools.partial(scatter_kernel, planes), out_shape=(jax....  59.7 us
    pallas_call x1, Pallas kernels, attend(): pl.pallas_call(attend_kernel, grid=(span // BLOCK,), in_specs=[whole(seg_...  8.16 us
    unnamed x7, local copies, waits for them, and re-layouts  4.56 us

profile of v4, /device:TPU:96, one launch (start us, length us, event | category | flops | bytes accessed | tf_op | source)
XLA Modules:
  0.0 148.1 jit_solution(3460782875916845250)
XLA Ops:
  0.6 75.0 %gather_plane.1 = (bf16[1024,1024]{1,0:T(8,128)(2,1)}, bf16[1024,1024]{1,0:T(8,128)(2,1)}, bf16[3072,128]{1,0:T(8,128)(2,1)}, bf16[3072,128]{1,0:T(8,128)(2,1)},...) custom-call(bf16[128,8192]{1,0:T(8,128)(2,1)} %q.1, ...), custom_call_target="tpu_custom_call" | custom-call | tf_op jit(solution)/shard_map/gather_plane/pallas_call | solution.py:401
  75.6 8.2 %attend.1 = (bf16[1024,1024]{1,0:T(8,128)(2,1)}, bf16[2048,128]{1,0:T(8,128)(2,1)}, bf16[2048,128]{1,0:T(8,128)(2,1)}) custom-call(s32[8,3072]{1,0:T(8,128)} %get-tuple-element.15.seg, f32[16,1024]{1,0:T(8,128)} %get-tuple-element.16.stats, bf16[1024,1024]{1,0:T(8,128)(2,1)} %get-tuple-element.17.q, bf16[1024,1024]{1,0:T(8,128)(2,1)} %get-tuple-element.18.g, ...), custom_call_target="tpu_custom_call" | custom-call | tf_op jit(solution)/shard_map/attend/pallas_call | solution.py:525
  83.8 59.7 %scatter_plane.1 = (bf16[128,8192]{1,0:T(8,128)(2,1)}, bf16[128,1024]{1,0:T(8,128)(2,1)}, bf16[128,1024]{1,0:T(8,128)(2,1)}) custom-call(bf16[1024,1024]{1,0:T(8,128)(2,1)} %get-tuple-element.24.dq, bf16[2048,128]{1,0:T(8,128)(2,1)} %get-tuple-element.25.dk_halo, bf16[2048,128]{1,0:T(8,128)(2,1)} %get-tuple-element.26.dv_halo, ...), custom_call_target="tpu_custom_call" | custom-call | tf_op jit(solution)/shard_map/scatter_plane/pallas_call | solution.py:645
  143.5 0.0 copy-start.1
  143.5 0.0 copy-start
  143.5 3.2 %copy.13 = bf16[128,8192]{1,0:T(8,128)(2,1)} copy(bf16[128,8192]{1,0:T(8,128)(2,1)} %get-tuple-element.30) | data formatting | bytes 4194304
  146.7 0.0 copy-done.1
  146.7 0.7 copy.14
  147.4 0.0 copy-done
  147.4 0.7 copy.15
Async XLA Ops:
  143.5 3.2 %copy-start.1 = (bf16[128,1024]{1,0:T(8,128)(2,1)S(1)}, bf16[128,1024]{1,0:T(8,128)(2,1)}, u32[]{:S(2)}) copy-start(bf16[128,1024]{1,0:T(8,128)(2,1)} %get-tuple-element.31) | copy-start | bytes 786436
  143.5 3.9 %copy-start = (bf16[128,1024]{1,0:T(8,128)(2,1)S(1)}, bf16[128,1024]{1,0:T(8,128)(2,1)}, u32[]{:S(2)}) copy-start(bf16[128,1024]{1,0:T(8,128)(2,1)} %get-tuple-element.32) | copy-start | bytes 786436

commit v5 on v4

v5 whole, which is shorter than its diff:
```python
import functools
import math

import jax
import jax.numpy as jnp
from jax import lax
from jax.experimental import pallas as pl
from jax.experimental.pallas import tpu as pltpu
from jax.sharding import PartitionSpec as P

D = 128
LOG2E = math.log2(math.e)
MESH = pl.DeviceIdType.MESH
PLANE = 8
PLANE_X = 4
HALO = 2
CHUNKS = 4
WHOLE = 2
ROUTE_SEMS = 10
BLOCK = 256
VMEM_LIMIT = 60 * 1024 * 1024


def dev(index):
    return {"seq": index}


def greet(me, plane, rank, planes, reach):
    barrier = pltpu.get_barrier_semaphore()
    for o in range(1, PLANE):
        peer = plane * PLANE + lax.rem(rank + o, PLANE)
        pl.semaphore_signal(barrier, inc=1, device_id=dev(peer), device_id_type=MESH)
    count = PLANE - 1
    for dz in range(1, reach + 1):
        up = plane + dz < planes
        down = plane >= dz

        @pl.when(up)
        def _():
            pl.semaphore_signal(barrier, inc=1, device_id=dev(me + dz * PLANE), device_id_type=MESH)

        @pl.when(down)
        def _():
            pl.semaphore_signal(barrier, inc=1, device_id=dev(me - dz * PLANE), device_id_type=MESH)

        count = count + up.astype(jnp.int32) + down.astype(jnp.int32)
    pl.semaphore_wait(barrier, count)


class Route:
    def __init__(self, x_first, plane, rank, source, target, stage, sems):
        self.x_first, self.plane = x_first, plane
        self.y, self.x = rank // PLANE_X, lax.rem(rank, PLANE_X)
        self.source, self.target, self.stage = source, target, stage
        self.send, self.recv = sems

    def rank(self, dy, dx):
        y = self.y if dy == 0 else 1 - self.y
        return y * PLANE_X + lax.rem(self.x + dx + PLANE_X, PLANE_X)

    def copy(self, n, source, target, peer):
        return pltpu.make_async_remote_copy(
            source, target, self.send.at[n], self.recv.at[n],
            device_id=dev(self.plane * PLANE + peer), device_id_type=MESH,
        )

    def first_leg(self, dx):
        peer = self.rank(0, dx) if self.x_first else self.rank(1, 0)
        return self.copy(dx - 1, self.source(self.rank(1, dx)), self.stage.at[dx - 1], peer)

    def second_leg(self, dx):
        if self.x_first:
            origin, peer = self.rank(0, -dx), self.rank(1, 0)
        else:
            origin, peer = self.rank(1, 0), self.rank(0, dx)
        return self.copy(2 + dx, self.stage.at[dx - 1], self.target(origin), peer)

    def straight(self, dx):
        peer = self.rank(0, dx) if dx else self.rank(1, 0)
        return self.copy(6 + dx, self.source(peer), self.target(self.rank(0, 0)), peer)

    def start_first(self):
        for dx in range(1, PLANE_X):
            self.first_leg(dx).start()

    def start_straight(self):
        for dx in range(PLANE_X):
            self.straight(dx).start()

    def pass_on(self):
        for dx in range(1, PLANE_X):
            self.first_leg(dx).wait_recv()
            self.second_leg(dx).start()

    def wait_arrivals(self):
        for dx in range(PLANE_X):
            origin = self.rank(0, -dx) if dx else self.rank(1, 0)
            self.copy(6 + dx, self.target(origin), self.target(origin), origin).wait_recv()
        for dx in range(1, PLANE_X):
            origin = self.rank(1, -dx)
            self.copy(2 + dx, self.target(origin), self.target(origin), origin).wait_recv()

    def wait_sends(self):
        for dx in range(1, PLANE_X):
            self.first_leg(dx).wait_send()
            self.second_leg(dx).wait_send()
        for dx in range(PLANE_X):
            self.straight(dx).wait_send()


def tile_terms(k_rows, v_rows, q_rows, g_rows, lse_row, delta_row, visible):
    nt = (((1,), (1,)), ((), ()))
    scores = lax.dot_general(k_rows, q_rows, nt, preferred_element_type=jnp.float32)
    weights = jnp.exp2(scores * (LOG2E / math.sqrt(D)) - lse_row)
    if visible is not None:
        weights = jnp.where(visible(), weights, 0.0)
    d_weights = lax.dot_general(v_rows, g_rows, nt, preferred_element_type=jnp.float32)
    dscore = (weights * (d_weights - delta_row)).astype(jnp.bfloat16)
    return weights.astype(jnp.bfloat16), dscore


def begins_at(ids, first):
    at = lax.broadcasted_iota(jnp.int32, ids.shape, 1)
    begins = (ids != pltpu.roll(ids, 1, 1)) & (at > first)
    found = jnp.where(begins, at, first)
    step = 1
    while step < ids.shape[1]:
        found = jnp.where(at >= step, jnp.maximum(found, pltpu.roll(found, step, 1)), found)
        step *= 2
    return found


def kernel(
    planes, q, g, o, k, v, seg, lse, grad_q, grad_k, grad_v,
    o_here, g_here, q_in, g_in, k_in, v_in, k_t, start, seg_here, seg_win, stats, stats_in,
    dk, dv, dq_t, dq_low, far_out, far_in, near_out, near_in, low, stage, stage_back,
    r_send, r_recv, b_send, b_recv, send, recv, kv_send, kv_recv, z_send, z_recv, local,
):
    rows = q.shape[0]
    span = rows * PLANE
    wide = q_in.shape[1]
    heads = wide // D
    me = lax.axis_index("seq")
    plane, rank = me // PLANE, lax.rem(me, PLANE)
    own = HALO * span
    blocks = span // BLOCK
    narrow = wide // CHUNKS
    per_chunk = narrow // D
    across = per_chunk * BLOCK
    inv_root = 1.0 / math.sqrt(D)

    def part(index, width):
        return pl.ds(pl.multiple_of(index * width, width), width)

    def own_part(s):
        return pl.ds(pl.multiple_of(own + s * rows, rows), rows)

    pieces = [
        (lambda p: seg_here, lambda s: seg_win.at[:, own_part(s)]),
        (lambda p: k.at[:, part(p, D)], lambda s: k_in.at[own_part(s), :]),
        (lambda p: v.at[:, part(p, D)], lambda s: v_in.at[own_part(s), :]),
        (lambda p: stats.at[part(p, 2 * heads), :], lambda s: stats_in.at[:, part(s, rows)]),
        (lambda p: q.at[:, part(p, wide)], lambda s: q_in.at[part(s, rows), :]),
        (lambda p: g.at[:, part(p, wide)], lambda s: g_in.at[part(s, rows), :]),
    ]
    last = 3

    def routes(c):
        made = []
        for n, (array, gathered) in enumerate(((q, q_in), (g, g_in))):
            def source(p, array=array):
                return array.at[:, pl.ds(pl.multiple_of(p * wide + c * narrow, narrow), narrow)]

            def target(s, gathered=gathered):
                return gathered.at[part(s, rows), part(c, narrow)]

            made.append(Route(
                n == 0, plane, rank, source, target, stage.at[n, c], (r_send.at[n, c], r_recv.at[n, c])
            ))
        return made

    def route_back(c):
        def source(p):
            return dq_low.at[part(p, rows), pl.ds(c * narrow, narrow)]

        def target(s):
            return grad_q.at[:, pl.ds(pl.multiple_of(s * wide + c * narrow, narrow), narrow)]

        return Route(c % 2 == 0, plane, rank, source, target, stage_back.at[c], (b_send.at[c], b_recv.at[c]))

    back = [route_back(c) for c in range(CHUNKS)]

    def own_copy(n):
        source, target = pieces[n]
        return pltpu.make_async_copy(source(rank), target(rank), local.at[n])

    def plane_copy(n, o):
        source, target = pieces[n]
        peer = lax.rem(rank + o, PLANE)
        return pltpu.make_async_remote_copy(
            source(peer), target(rank), send.at[n, o - 1], recv.at[n, o - 1],
            device_id=dev(plane * PLANE + peer), device_id_type=MESH,
        )

    def arrival(n, o):
        source, target = pieces[n]
        origin = lax.rem(rank + PLANE - o, PLANE)
        return pltpu.make_async_remote_copy(
            source(rank), target(origin), send.at[n, o - 1], recv.at[n, o - 1],
            device_id=dev(plane * PLANE + origin), device_id_type=MESH,
        )

    def kv_copy(n, o, origin):
        peer = lax.rem(rank + o, PLANE)
        return pltpu.make_async_remote_copy(
            low.at[n, part(peer, rows), :], (grad_k, grad_v)[n].at[:, part(origin, D)],
            kv_send.at[n, o - 1], kv_recv.at[n, o - 1],
            device_id=dev(plane * PLANE + peer), device_id_type=MESH,
        )

    def z_copy(n, source, target, planes_on):
        return pltpu.make_async_remote_copy(
            source, target, z_send.at[n], z_recv.at[n],
            device_id=dev(me + planes_on * PLANE), device_id_type=MESH,
        )

    def seg_copy(dz):
        return z_copy(dz - 1, seg_win.at[:, pl.ds(own, span)], seg_win.at[:, pl.ds(own - dz * span, span)], dz)

    def halo_copy(n, dz):
        win = (k_in, v_in)[n]
        held, there = pl.ds(own - (dz - 1) * span, span), pl.ds(own - dz * span, span)
        return z_copy(2 * dz + n, win.at[held, :], win.at[there, :], 1)

    def far_copy(n):
        return z_copy(6 + n, far_out.at[n], far_in.at[n], -1)

    def near_copy(n):
        return z_copy(8 + n, near_out.at[n], near_in.at[n], -1)

    def start_chunk(c):
        for path in routes(c):
            path.start_first()
        for path in routes(c):
            path.start_straight()

    def pass_on(c):
        for path in routes(c):
            path.pass_on()

    def start_back(c):
        back[c].start_first()
        back[c].start_straight()

    def transpose_keys(dz):
        held = pl.ds(own - dz * span, span)
        k_t[:, held] = k_in[held, :].T

    def take_halo(dz):
        held = pl.ds(own - dz * span, span)

        @pl.when(plane >= dz)
        def _():
            for n in range(2):
                halo_copy(n, dz).wait_recv()

        @pl.when(plane < dz)
        def _():
            k_in[held, :] = jnp.zeros((span, D), k_in.dtype)
            v_in[held, :] = jnp.zeros((span, D), v_in.dtype)

        if dz < HALO:
            @pl.when((plane >= dz) & (plane + 1 < planes))
            def _():
                for n in range(2):
                    halo_copy(n, dz + 1).start()
        transpose_keys(dz)

    def tiles(c, dz, first):
        operands = []
        for i in range(blocks):
            here = pl.ds(i * BLOCK, BLOCK)

            def stacked(ref, here=here):
                return jnp.concatenate(
                    [ref[here, pl.ds(pl.multiple_of(c * narrow + h * D, D), D)] for h in range(per_chunk)], axis=0
                )

            def in_line(at, here=here):
                return jnp.concatenate(
                    [stats_in[pl.ds(at + c * per_chunk + h, 1), here] for h in range(per_chunk)], axis=1
                )

            start_row = jnp.concatenate([start[0:1, here]] * per_chunk, axis=1)
            operands.append((stacked(q_in), stacked(g_in), in_line(0) * LOG2E, in_line(heads), start_row))
        totals = [None] * blocks
        down = lax.broadcasted_iota(jnp.int32, (BLOCK, across), 0)
        query_at = lax.rem(lax.broadcasted_iota(jnp.int32, (1, across), 1), BLOCK)
        for before in range(HALO * blocks + 1):
            for i in range(blocks):
                j = HALO * blocks + i - before
                if j // blocks != HALO - dz:
                    continue
                there = pl.ds(j * BLOCK, BLOCK)
                q_rows, g_rows, lse_row, delta_row, start_row = operands[i]

                def visible(j=j, before=before, start_row=start_row):
                    seen = down >= start_row - j * BLOCK
                    return seen & (down <= query_at) if before == 0 else seen

                weights, dscore = tile_terms(
                    k_in[there, :], v_in[there, :], q_rows, g_rows, lse_row, delta_row, visible
                )
                dv[there, :] += jnp.dot(weights, g_rows, preferred_element_type=jnp.float32)
                dk[there, :] += jnp.dot(dscore, q_rows, preferred_element_type=jnp.float32)
                term = jnp.dot(k_t[:, there], dscore, preferred_element_type=jnp.float32)
                totals[i] = term if totals[i] is None else totals[i] + term
        for i in range(blocks):
            if first:
                dq_t[pl.ds(i * D, D), part(c, across)] = totals[i]
            else:
                dq_t[pl.ds(i * D, D), part(c, across)] += totals[i]

    def finish_queries(c):
        for i in range(blocks):
            for h in range(per_chunk):
                total = dq_t[pl.ds(i * D, D), pl.ds(pl.multiple_of(c * across + h * BLOCK, BLOCK), BLOCK)]
                dq_low[pl.ds(i * BLOCK, BLOCK), pl.ds(pl.multiple_of(c * narrow + h * D, D), D)] = (
                    total.T * inv_root
                ).astype(dq_low.dtype)

    load_o = pltpu.make_async_copy(o, o_here, local.at[6])
    load_g = pltpu.make_async_copy(g, g_here, local.at[7])
    load_o.start()
    load_g.start()
    seg_here[...] = jnp.broadcast_to(seg[...], seg_here.shape)
    greet(me, plane, rank, planes, HALO)
    for n in range(last):
        for o_at in range(1, PLANE):
            plane_copy(n, o_at).start()
        own_copy(n).start()
    start_chunk(0)
    start_chunk(1)
    own_copy(4).start()
    own_copy(5).start()

    load_o.wait()
    load_g.wait()

    @pl.loop(0, PLANE)
    def _(p):
        sums = []
        for h in range(heads):
            features = pl.ds(pl.multiple_of(p * wide + h * D, D), D)
            product = o_here[:, features].astype(jnp.float32) * g_here[:, features].astype(jnp.float32)
            sums.append(jnp.sum(product.T, axis=0, keepdims=True))
        stats[part(p * 2, heads), :] = lse[part(p, heads), :]
        stats[part(p * 2 + 1, heads), :] = jnp.concatenate(sums, axis=0)

    for o_at in range(1, PLANE):
        plane_copy(last, o_at).start()
    own_copy(last).start()

    for n in range(last):
        own_copy(n).wait()
        for o_at in range(1, PLANE):
            arrival(n, o_at).wait_recv()
        if n == 0:
            for dz in range(1, HALO + 1):
                @pl.when(plane + dz < planes)
                def _():
                    seg_copy(dz).start()
        else:
            @pl.when(plane + 1 < planes)
            def _():
                halo_copy(n - 1, 1).start()
    pass_on(0)
    dk[...] = jnp.zeros_like(dk)
    dv[...] = jnp.zeros_like(dv)
    transpose_keys(0)
    for dz in range(1, HALO + 1):
        @pl.when(plane >= dz)
        def _():
            seg_copy(dz).wait_recv()
    start[...] = begins_at(seg_win[...], own - jnp.minimum(plane, HALO) * span)[:, own:]
    own_copy(last).wait()
    own_copy(4).wait()
    own_copy(5).wait()
    for o_at in range(1, PLANE):
        arrival(last, o_at).wait_recv()

    @pl.loop(0, WHOLE)
    def _(c):
        @pl.when(c + 2 < CHUNKS)
        def _():
            start_chunk(c + 2)

        pass_on(c + 1)
        for path in routes(c):
            path.wait_arrivals()
        for dz in range(HALO + 1):
            if dz > 0:
                @pl.when(c == 0)
                def _():
                    take_halo(dz)

            tiles(c, dz, dz == 0)
        finish_queries(c)
        for n in range(WHOLE):
            @pl.when(c == n)
            def _():
                start_back(n)

    @pl.loop(WHOLE, CHUNKS)
    def _(c):
        @pl.when(c + 1 < CHUNKS)
        def _():
            pass_on(c + 1)

        for path in routes(c):
            path.wait_arrivals()
        tiles(c, 2, True)

    far_out[0] = (dk[:span, :] * inv_root).astype(far_out.dtype)
    far_out[1] = dv[:span, :].astype(far_out.dtype)

    @pl.when(plane >= 2)
    def _():
        for n in range(2):
            far_copy(n).start()

    for n in range(WHOLE):
        back[n].pass_on()

    @pl.loop(WHOLE, CHUNKS)
    def _(c):
        tiles(c, 1, False)

    dk[pl.ds(span, span), :] = dk[pl.ds(span, span), :] * inv_root
    takes_far = (plane >= 1) & (plane + 1 < planes)

    @pl.when(takes_far)
    def _():
        for n in range(2):
            far_copy(n).wait_recv()
            total = (dk, dv)[n]
            near_out[n] = (total[pl.ds(span, span), :] + far_in[n].astype(jnp.float32)).astype(near_out.dtype)

    @pl.when(plane + 1 >= planes)
    def _():
        for n in range(2):
            near_out[n] = (dk, dv)[n][pl.ds(span, span), :].astype(near_out.dtype)

    @pl.when(plane >= 1)
    def _():
        for n in range(2):
            near_copy(n).start()

    for c in range(WHOLE, CHUNKS):
        tiles(c, 0, False)
        finish_queries(c)
        start_back(c)

    dk[pl.ds(own, span), :] = dk[pl.ds(own, span), :] * inv_root
    own_back = pltpu.make_async_copy(dq_low.at[part(rank, rows), :], grad_q.at[:, part(rank, wide)], local.at[4])
    own_back.start()
    back[WHOLE].pass_on()
    own_kv = []
    for n in range(2):
        total = (dk, dv)[n]

        @pl.when(plane + 1 < planes)
        def _():
            near_copy(n).wait_recv()
            low[n] = (total[pl.ds(own, span), :] + near_in[n].astype(jnp.float32)).astype(low.dtype)

        @pl.when(plane + 1 >= planes)
        def _():
            low[n] = total[pl.ds(own, span), :].astype(low.dtype)

        for o_at in range(1, PLANE):
            kv_copy(n, o_at, rank).start()
        own_kv.append(pltpu.make_async_copy(
            low.at[n, part(rank, rows), :], (grad_k, grad_v)[n].at[:, part(rank, D)], local.at[6 + n]
        ))
        own_kv[n].start()
    for c in range(WHOLE + 1, CHUNKS):
        back[c].pass_on()

    own_back.wait()
    for n in range(2):
        own_kv[n].wait()
    for c in range(CHUNKS):
        for path in routes(c):
            path.wait_sends()
        back[c].wait_arrivals()
        back[c].wait_sends()
    for o_at in range(1, PLANE):
        for n in range(last + 1):
            plane_copy(n, o_at).wait_send()
        origin = lax.rem(rank + PLANE - o_at, PLANE)
        for n in range(2):
            kv_copy(n, o_at, origin).wait()
    for dz in range(1, HALO + 1):
        @pl.when(plane + dz < planes)
        def _():
            seg_copy(dz).wait_send()

        @pl.when((plane + 1 < planes) & (plane + 1 >= dz))
        def _():
            for n in range(2):
                halo_copy(n, dz).wait_send()

    @pl.when(plane >= 2)
    def _():
        for n in range(2):
            far_copy(n).wait_send()

    @pl.when(plane >= 1)
    def _():
        for n in range(2):
            near_copy(n).wait_send()


def on_device(q, k, v, o, g, lse, segments):
    planes = lax.axis_size("seq") // PLANE
    rows = q.shape[0]
    span = rows * PLANE
    heads = lse.shape[0] // PLANE
    wide = heads * D
    window = (HALO + 1) * span
    any_space = pl.BlockSpec(memory_space=pl.ANY)
    vmem = pl.BlockSpec(memory_space=pltpu.VMEM)
    low, wider, sems = jnp.bfloat16, jnp.float32, pltpu.SemaphoreType.DMA
    return pl.pallas_call(
        functools.partial(kernel, planes),
        out_shape=(
            jax.ShapeDtypeStruct(q.shape, low),
            jax.ShapeDtypeStruct(k.shape, low),
            jax.ShapeDtypeStruct(v.shape, low),
        ),
        in_specs=[any_space] * 5 + [vmem] * 2,
        out_specs=(any_space,) * 3,
        scratch_shapes=[
            pltpu.VMEM(o.shape, low),
            pltpu.VMEM(g.shape, low),
            pltpu.VMEM((span, wide), low),
            pltpu.VMEM((span, wide), low),
            pltpu.VMEM((window, D), low),
            pltpu.VMEM((window, D), low),
            pltpu.VMEM((D, window), low),
            pltpu.VMEM((8, span), jnp.int32),
            pltpu.VMEM((8, rows), jnp.int32),
            pltpu.VMEM((8, window), jnp.int32),
            pltpu.VMEM((2 * heads * PLANE, rows), wider),
            pltpu.VMEM((2 * heads, span), wider),
            pltpu.VMEM((window, D), wider),
            pltpu.VMEM((window, D), wider),
            pltpu.VMEM((span // BLOCK * D, heads * BLOCK), wider),
            pltpu.VMEM((span, wide), low),
            pltpu.VMEM((2, span, D), low),
            pltpu.VMEM((2, span, D), low),
            pltpu.VMEM((2, span, D), low),
            pltpu.VMEM((2, span, D), low),
            pltpu.VMEM((2, span, D), low),
            pltpu.VMEM((2, CHUNKS, PLANE_X - 1, rows, wide // CHUNKS), low),
            pltpu.VMEM((CHUNKS, PLANE_X - 1, rows, wide // CHUNKS), low),
            sems((2, CHUNKS, ROUTE_SEMS)),
            sems((2, CHUNKS, ROUTE_SEMS)),
            sems((CHUNKS, ROUTE_SEMS)),
            sems((CHUNKS, ROUTE_SEMS)),
            sems((4, PLANE - 1)),
            sems((4, PLANE - 1)),
            sems((2, PLANE - 1)),
            sems((2, PLANE - 1)),
            sems((10,)),
            sems((10,)),
            sems((8,)),
        ],
        compiler_params=pltpu.CompilerParams(
            collective_id=0, has_side_effects=True, vmem_limit_bytes=VMEM_LIMIT
        ),
        name="attention_back",
    )(q, g, o, k, v, segments[None, :], lse)


def solution(mesh):
    rows = P(("dp", "seq"), None)
    in_specs = (rows, rows, rows, rows, rows, P(None, ("dp", "seq")), P(("dp", "seq")))
    return jax.shard_map(
        on_device, mesh=mesh, in_specs=in_specs, out_specs=(rows, rows, rows), check_vma=False
    )
```

time: 150 us -> 123 us (0.82)
  Pallas kernels: 143 us -> 117 us
    pallas_call x3 -> x1, Pallas kernels: 143 us -> 117 us  [on_device(): pl.pallas_call(functools.partial(kernel, planes), out_shape=(jax.ShapeDty...]
where the time goes in v5:
time: 123 us; the launch traced here: 122 us
  Pallas kernels  117 us (95%)
  local copies, waits for them, and re-layouts  4.56 us (4%)
    pallas_call x1, Pallas kernels, on_device(): pl.pallas_call(functools.partial(kernel, planes), out_shape=(jax.ShapeDty...  117 us
    unnamed x7, local copies, waits for them, and re-layouts  4.56 us

profile of v5, /device:TPU:96, one launch (start us, length us, event | category | flops | bytes accessed | tf_op | source)
XLA Modules:
  0.0 122.3 jit_solution(13111020815267387505)
XLA Ops:
  0.6 117.0 %attention_back.1 = (bf16[128,8192]{1,0:T(8,128)(2,1)}, bf16[128,1024]{1,0:T(8,128)(2,1)}, bf16[128,1024]{1,0:T(8,128)(2,1)}) custom-call(bf16[128,8192]{1,0:T(8,128)(2,1)} %q.1, bf16[128,8192]{1,0:T(8,128)(2,1)} %g.1, bf16[128,8192]{1,0:T(8,128)(2,1)} %o.1, bf16[128,1024]{1,0:T(8,128)(2,1)} %k.1, bf16[128,1024]{1,0:T(8,128)(2,1)} %v.1, s32[1,128]{1,0:T(1,128)} %bitcast.1, ...), custom_call_target="tpu_custom_call" | custom-call | tf_op jit(solution)/shard_map/attention_back/pallas_call | solution.py:535
  117.7 0.0 copy-start.1
  117.7 0.0 copy-start
  117.7 3.2 %copy.13 = bf16[128,8192]{1,0:T(8,128)(2,1)} copy(bf16[128,8192]{1,0:T(8,128)(2,1)} %get-tuple-element.6) | data formatting | bytes 4194304
  120.9 0.0 copy-done.1
  120.9 0.7 copy.14
  121.6 0.0 copy-done
  121.6 0.7 copy.15
Async XLA Ops:
  117.7 3.2 %copy-start.1 = (bf16[128,1024]{1,0:T(8,128)(2,1)S(1)}, bf16[128,1024]{1,0:T(8,128)(2,1)}, u32[]{:S(2)}) copy-start(bf16[128,1024]{1,0:T(8,128)(2,1)} %get-tuple-element.7) | copy-start | bytes 786436
  117.7 3.9 %copy-start = (bf16[128,1024]{1,0:T(8,128)(2,1)S(1)}, bf16[128,1024]{1,0:T(8,128)(2,1)}, u32[]{:S(2)}) copy-start(bf16[128,1024]{1,0:T(8,128)(2,1)} %get-tuple-element.8) | copy-start | bytes 786436

commit v6 on v5

--- a/solution.py
+++ b/solution.py
@@ -340,27 +340,8 @@
             plane_copy(n, o_at).start()
         own_copy(n).start()
     start_chunk(0)
-    start_chunk(1)
     own_copy(4).start()
     own_copy(5).start()
-
-    load_o.wait()
-    load_g.wait()
-
-    @pl.loop(0, PLANE)
-    def _(p):
-        sums = []
-        for h in range(heads):
-            features = pl.ds(pl.multiple_of(p * wide + h * D, D), D)
-            product = o_here[:, features].astype(jnp.float32) * g_here[:, features].astype(jnp.float32)
-            sums.append(jnp.sum(product.T, axis=0, keepdims=True))
-        stats[part(p * 2, heads), :] = lse[part(p, heads), :]
-        stats[part(p * 2 + 1, heads), :] = jnp.concatenate(sums, axis=0)
-
-    for o_at in range(1, PLANE):
-        plane_copy(last, o_at).start()
-    own_copy(last).start()
-
     for n in range(last):
         own_copy(n).wait()
         for o_at in range(1, PLANE):
@@ -375,6 +356,24 @@
             def _():
                 halo_copy(n - 1, 1).start()
     pass_on(0)
+
+    load_o.wait()
+    load_g.wait()
+
+    @pl.loop(0, PLANE)
+    def _(p):
+        sums = []
+        for h in range(heads):
+            features = pl.ds(pl.multiple_of(p * wide + h * D, D), D)
+            product = o_here[:, features].astype(jnp.float32) * g_here[:, features].astype(jnp.float32)
+            sums.append(jnp.sum(product.T, axis=0, keepdims=True))
+        stats[part(p * 2, heads), :] = lse[part(p, heads), :]
+        stats[part(p * 2 + 1, heads), :] = jnp.concatenate(sums, axis=0)
+
+    for o_at in range(1, PLANE):
+        plane_copy(last, o_at).start()
+    own_copy(last).start()
+    start_chunk(1)
     dk[...] = jnp.zeros_like(dk)
     dv[...] = jnp.zeros_like(dv)
     transpose_keys(0)
@@ -391,11 +390,6 @@
 
     @pl.loop(0, WHOLE)
     def _(c):
-        @pl.when(c + 2 < CHUNKS)
-        def _():
-            start_chunk(c + 2)
-
-        pass_on(c + 1)
         for path in routes(c):
             path.wait_arrivals()
         for dz in range(HALO + 1):
@@ -405,6 +399,15 @@
                     take_halo(dz)
 
             tiles(c, dz, dz == 0)
+            if dz == 0:
+                pass_on(c + 1)
+                start_chunk(c + 2)
+            if dz == 1:
+                @pl.when(c == WHOLE - 1)
+                def _():
+                    pass_on(WHOLE + 1)
+                    back[0].pass_on()
+
         finish_queries(c)
         for n in range(WHOLE):
             @pl.when(c == n)
@@ -413,10 +416,6 @@
 
     @pl.loop(WHOLE, CHUNKS)
     def _(c):
-        @pl.when(c + 1 < CHUNKS)
-        def _():
-            pass_on(c + 1)
-
         for path in routes(c):
             path.wait_arrivals()
         tiles(c, 2, True)
@@ -429,8 +428,7 @@
         for n in range(2):
             far_copy(n).start()
 
-    for n in range(WHOLE):
-        back[n].pass_on()
+    back[1].pass_on()
 
     @pl.loop(WHOLE, CHUNKS)
     def _(c):
@@ -522,6 +520,11 @@
             near_copy(n).wait_send()
 
 
+def hand_over(*refs):
+    for source, target in zip(refs[:3], refs[3:]):
+        target[...] = source[...]
+
+
 def on_device(q, k, v, o, g, lse, segments):
     planes = lax.axis_size("seq") // PLANE
     rows = q.shape[0]
@@ -532,7 +535,7 @@
     any_space = pl.BlockSpec(memory_space=pl.ANY)
     vmem = pl.BlockSpec(memory_space=pltpu.VMEM)
     low, wider, sems = jnp.bfloat16, jnp.float32, pltpu.SemaphoreType.DMA
-    return pl.pallas_call(
+    grads = pl.pallas_call(
         functools.partial(kernel, planes),
         out_shape=(
             jax.ShapeDtypeStruct(q.shape, low),
@@ -582,6 +585,16 @@
         ),
         name="attention_back",
     )(q, g, o, k, v, segments[None, :], lse)
+    cut = [pl.BlockSpec((rows // 4, x.shape[1]), lambda i: (i, 0)) for x in grads]
+    return pl.pallas_call(
+        hand_over,
+        grid=(4,),
+        in_specs=cut,
+        out_specs=cut,
+        out_shape=[jax.ShapeDtypeStruct(x.shape, x.dtype) for x in grads],
+        compiler_params=pltpu.CompilerParams(vmem_limit_bytes=VMEM_LIMIT),
+        name="hand_over",
+    )(*grads)
 
 
 def solution(mesh):

time: 123 us -> 116 us (0.943)
  local copies, waits for them, and re-layouts: 4.56 us -> 0 us
  Pallas kernels: 117 us -> 115 us
    pallas_call x1, Pallas kernels: 117 us -> 111 us  [on_device(): pl.pallas_call(functools.partial(kernel, planes), out_shape=(jax.ShapeDty...]
    unnamed x7 -> x0, local copies, waits for them, and re-layouts: 4.56 us -> none
    pallas_call x0 -> x1, Pallas kernels: none -> 3.94 us  [on_device(): pl.pallas_call(hand_over, grid=(4,), in_specs=cut, out_specs=cut, out_sha...]
where the time goes in v6:
time: 116 us; the launch traced here: 115 us
  Pallas kernels  115 us (99%)
    pallas_call x1, Pallas kernels, on_device(): pl.pallas_call(functools.partial(kernel, planes), out_shape=(jax.ShapeDty...  111 us
    pallas_call x1, Pallas kernels, on_device(): pl.pallas_call(hand_over, grid=(4,), in_specs=cut, out_specs=cut, out_sha...  3.94 us

profile of v6, /device:TPU:96, one launch (start us, length us, event | category | flops | bytes accessed | tf_op | source)
XLA Modules:
  0.0 115.3 jit_solution(18377265549513867721)
XLA Ops:
  0.6 110.7 %attention_back.1 = (bf16[128,8192]{1,0:T(8,128)(2,1)}, bf16[128,1024]{1,0:T(8,128)(2,1)}, bf16[128,1024]{1,0:T(8,128)(2,1)}) custom-call(bf16[128,8192]{1,0:T(8,128)(2,1)} %q.1, bf16[128,8192]{1,0:T(8,128)(2,1)} %g.1, bf16[128,8192]{1,0:T(8,128)(2,1)} %o.1, bf16[128,1024]{1,0:T(8,128)(2,1)} %k.1, bf16[128,1024]{1,0:T(8,128)(2,1)} %v.1, s32[1,128]{1,0:T(1,128)} %bitcast.1, ...), custom_call_target="tpu_custom_call" | custom-call | tf_op jit(solution)/shard_map/attention_back/pallas_call | solution.py:538
  111.4 3.9 %hand_over.1 = (bf16[128,8192]{1,0:T(8,128)(2,1)}, bf16[128,1024]{1,0:T(8,128)(2,1)}, bf16[128,1024]{1,0:T(8,128)(2,1)}) custom-call(bf16[128,8192]{1,0:T(8,128)(2,1)} %get-tuple-element.6.refs_0_, bf16[128,1024]{1,0:T(8,128)(2,1)} %get-tuple-element.7.refs_1_, bf16[128,1024]{1,0:T(8,128)(2,1)} %get-tuple-element.8.refs_2_), custom_call_target="tpu_custom_call" | custom-call | tf_op jit(solution)/shard_map/hand_over/pallas_call | solution.py:589

commit v7 on v6

--- a/solution.py
+++ b/solution.py
@@ -15,6 +15,7 @@
 PLANE_X = 4
 HALO = 2
 CHUNKS = 4
+PIECES = 4
 WHOLE = 2
 ROUTE_SEMS = 10
 BLOCK = 256
@@ -336,10 +337,14 @@
     seg_here[...] = jnp.broadcast_to(seg[...], seg_here.shape)
     greet(me, plane, rank, planes, HALO)
     for n in range(last):
+        if n == 1:
+            for path in routes(0):
+                path.start_first()
         for o_at in range(1, PLANE):
             plane_copy(n, o_at).start()
         own_copy(n).start()
-    start_chunk(0)
+    for path in routes(0):
+        path.start_straight()
     own_copy(4).start()
     own_copy(5).start()
     for n in range(last):
@@ -351,11 +356,11 @@
                 @pl.when(plane + dz < planes)
                 def _():
                     seg_copy(dz).start()
+            pass_on(0)
         else:
             @pl.when(plane + 1 < planes)
             def _():
                 halo_copy(n - 1, 1).start()
-    pass_on(0)
 
     load_o.wait()
     load_g.wait()
@@ -521,8 +526,23 @@
 
 
 def hand_over(*refs):
-    for source, target in zip(refs[:3], refs[3:]):
-        target[...] = source[...]
+    sources, targets, held, arrived, left = refs[:3], refs[3:6], refs[6:9], refs[9], refs[10]
+    copies = []
+    for n in range(3):
+        rows = sources[n].shape[0] // PIECES
+        for m in range(PIECES):
+            at = pl.ds(m * rows, rows)
+            copies.append((
+                pltpu.make_async_copy(sources[n].at[at, :], held[n].at[at, :], arrived.at[n, m]),
+                pltpu.make_async_copy(held[n].at[at, :], targets[n].at[at, :], left.at[n, m]),
+            ))
+    for load, _ in copies:
+        load.start()
+    for load, store in copies:
+        load.wait()
+        store.start()
+    for _, store in copies:
+        store.wait()
 
 
 def on_device(q, k, v, o, g, lse, segments):
@@ -585,12 +605,11 @@
         ),
         name="attention_back",
     )(q, g, o, k, v, segments[None, :], lse)
-    cut = [pl.BlockSpec((rows // 4, x.shape[1]), lambda i: (i, 0)) for x in grads]
     return pl.pallas_call(
         hand_over,
-        grid=(4,),
-        in_specs=cut,
-        out_specs=cut,
+        in_specs=[any_space] * 3,
+        out_specs=[any_space] * 3,
+        scratch_shapes=[pltpu.VMEM(x.shape, x.dtype) for x in grads] + [sems((3, PIECES)), sems((3, PIECES))],
         out_shape=[jax.ShapeDtypeStruct(x.shape, x.dtype) for x in grads],
         compiler_params=pltpu.CompilerParams(vmem_limit_bytes=VMEM_LIMIT),
         name="hand_over",

time: 116 us -> 114 us (0.983)
  Pallas kernels: 115 us -> 113 us
    pallas_call x1, Pallas kernels: 3.94 us -> 2.72 us  [on_device(): pl.pallas_call(hand_over, in_specs=[any_space] * 3, out_specs=[any_space]...]
where the time goes in v7:
time: 114 us
  Pallas kernels  113 us (99%)
    pallas_call x1, Pallas kernels, on_device(): pl.pallas_call(functools.partial(kernel, planes), out_shape=(jax.ShapeDty...  110 us
    pallas_call x1, Pallas kernels, on_device(): pl.pallas_call(hand_over, in_specs=[any_space] * 3, out_specs=[any_space]...  2.72 us

profile of v7, /device:TPU:96, one launch (start us, length us, event | category | flops | bytes accessed | tf_op | source)
XLA Modules:
  0.0 113.9 jit_solution(4787006776546638624)
XLA Ops:
  0.6 110.3 %attention_back.1 = (bf16[128,8192]{1,0:T(8,128)(2,1)}, bf16[128,1024]{1,0:T(8,128)(2,1)}, bf16[128,1024]{1,0:T(8,128)(2,1)}) custom-call(bf16[128,8192]{1,0:T(8,128)(2,1)} %q.1, bf16[128,8192]{1,0:T(8,128)(2,1)} %g.1, bf16[128,8192]{1,0:T(8,128)(2,1)} %o.1, bf16[128,1024]{1,0:T(8,128)(2,1)} %k.1, bf16[128,1024]{1,0:T(8,128)(2,1)} %v.1, s32[1,128]{1,0:T(1,128)} %bitcast.1, ...), custom_call_target="tpu_custom_call" | custom-call | tf_op jit(solution)/shard_map/attention_back/pallas_call | solution.py:558
  111.0 2.7 %hand_over.1 = (bf16[128,8192]{1,0:T(8,128)(2,1)}, bf16[128,1024]{1,0:T(8,128)(2,1)}, bf16[128,1024]{1,0:T(8,128)(2,1)}) custom-call(bf16[128,8192]{1,0:T(8,128)(2,1)} %get-tuple-element.6.refs_0_, bf16[128,1024]{1,0:T(8,128)(2,1)} %get-tuple-element.7.refs_1_, bf16[128,1024]{1,0:T(8,128)(2,1)} %get-tuple-element.8.refs_2_), custom_call_target="tpu_custom_call" | custom-call | tf_op jit(solution)/shard_map/hand_over/pallas_call | solution.py:608

commit v8 on v7

--- a/solution.py
+++ b/solution.py
@@ -461,13 +461,14 @@
 
     for c in range(WHOLE, CHUNKS):
         tiles(c, 0, False)
+        if c > WHOLE:
+            back[c - 1].pass_on()
         finish_queries(c)
         start_back(c)
 
     dk[pl.ds(own, span), :] = dk[pl.ds(own, span), :] * inv_root
     own_back = pltpu.make_async_copy(dq_low.at[part(rank, rows), :], grad_q.at[:, part(rank, wide)], local.at[4])
     own_back.start()
-    back[WHOLE].pass_on()
     own_kv = []
     for n in range(2):
         total = (dk, dv)[n]

time: 114 us -> 116 us (1.018)
  Pallas kernels: 113 us -> 115 us
    pallas_call x1, Pallas kernels: 110 us -> 112 us  [on_device(): pl.pallas_call(functools.partial(kernel, planes), out_shape=(jax.ShapeDty...]
where the time goes in v8:
time: 116 us
  Pallas kernels  115 us (99%)
    pallas_call x1, Pallas kernels, on_device(): pl.pallas_call(functools.partial(kernel, planes), out_shape=(jax.ShapeDty...  112 us
    pallas_call x1, Pallas kernels, on_device(): pl.pallas_call(hand_over, in_specs=[any_space] * 3, out_specs=[any_space]...  2.72 us

profile of v8, /device:TPU:96, one launch (start us, length us, event | category | flops | bytes accessed | tf_op | source)
XLA Modules:
  0.0 115.6 jit_solution(1048425986426204879)
XLA Ops:
  0.6 112.1 %attention_back.1 = (bf16[128,8192]{1,0:T(8,128)(2,1)}, bf16[128,1024]{1,0:T(8,128)(2,1)}, bf16[128,1024]{1,0:T(8,128)(2,1)}) custom-call(bf16[128,8192]{1,0:T(8,128)(2,1)} %q.1, bf16[128,8192]{1,0:T(8,128)(2,1)} %g.1, bf16[128,8192]{1,0:T(8,128)(2,1)} %o.1, bf16[128,1024]{1,0:T(8,128)(2,1)} %k.1, bf16[128,1024]{1,0:T(8,128)(2,1)} %v.1, s32[1,128]{1,0:T(1,128)} %bitcast.1, ...), custom_call_target="tpu_custom_call" | custom-call | tf_op jit(solution)/shard_map/attention_back/pallas_call | solution.py:559
  112.7 2.7 %hand_over.1 = (bf16[128,8192]{1,0:T(8,128)(2,1)}, bf16[128,1024]{1,0:T(8,128)(2,1)}, bf16[128,1024]{1,0:T(8,128)(2,1)}) custom-call(bf16[128,8192]{1,0:T(8,128)(2,1)} %get-tuple-element.6.refs_0_, bf16[128,1024]{1,0:T(8,128)(2,1)} %get-tuple-element.7.refs_1_, bf16[128,1024]{1,0:T(8,128)(2,1)} %get-tuple-element.8.refs_2_), custom_call_target="tpu_custom_call" | custom-call | tf_op jit(solution)/shard_map/hand_over/pallas_call | solution.py:609
